TPU v7x, 512 devices: a whole 4x4x16 slice. The times are simulated.
512 devices in a mesh: ia: 8 (over z_lo, core), ja: 16 (over z_hi, y), ka: 4 (over x).
Axes of the slice: x: 4, y: 4, z: 16 (z_hi: 4, z_lo: 4; z = z_hi * 4 + z_lo), core: 2. Of those that a mesh axis runs over, the one named last changes fastest.
Arguments:
- factor_a: bfloat16 [8, 2048, 128], P('ia', ('ja', 'ka')), may hold values from -6 to 6
- factor_b: bfloat16 [16, 1024, 128], P('ja', ('ia', 'ka')), may hold values from -6 to 6
- factor_c: bfloat16 [4, 4096, 128], P('ka', ('ia', 'ja')), may hold values from -6 to 6
- observed: bfloat16 [8, 16, 4, 36, 32, 1024], P('ia', 'ja', 'ka'), may hold values from -6 to 6
- coords: int32 [3, 8, 16, 4, 36], P(None, 'ia', 'ja', 'ka'), may hold values from 0 to 127, as said below
- counts: int32 [8, 16, 4], P('ia', 'ja', 'ka'), may hold values from 18 to 36, as said below
Outputs:
- residual: bfloat16 [8, 16, 4, 36, 32, 1024], P('ia', 'ja', 'ka')
- grad_a: float32 [8, 2048, 128], P('ia', ('ja', 'ka'))
- grad_b: float32 [16, 1024, 128], P('ja', ('ia', 'ka'))
- grad_c: float32 [4, 4096, 128], P('ka', ('ia', 'ja'))
Inputs may be any that keep to these rules, and one draw needn't show every extreme that they name: `coords`: component 0 lies in 0 to 63, component 1 in 0 to 31, component 2 in 0 to 127; several slots may name the same block. Slots 0 to counts - 1 of a device are live; some device has all 36 slots live.
All inputs are finite; a program needn't handle non-finite values.
Results may differ from a plain program's by a relative error of at most 0.019.
Values may be sent and summed in bfloat16 or wider, within the bound.
No kernel may reach another device: no remote copies, remote signals or barrier semaphores. Data moves between devices by JAX's collectives and lax.ppermute only.
A program may use at most 64 MiB of HBM per device.

v0:
```python
import jax
import jax.numpy as jnp
from jax import lax
from jax.sharding import PartitionSpec as P


def block_terms(tile_a, tile_b, tile_c, observed_blocks, weight):
    flt = jnp.float32
    groups, extent, columns = tile_a.shape
    pair_bc = (tile_b[:, :, None, :] * tile_c[:, None, :, :]).reshape(
        groups, extent * extent, columns
    )
    pair_ac = tile_a[:, :, None, :] * tile_c[:, None, :, :]
    pair_ab = tile_a[:, :, None, :] * tile_b[:, None, :, :]
    model = jnp.einsum("gar,gxr->gax", tile_a, pair_bc, preferred_element_type=flt)
    resid = (weight[:, None, None] * (model - observed_blocks.astype(flt))).astype(jnp.bfloat16)
    term_a = jnp.einsum("gax,gxr->gar", resid, pair_bc, preferred_element_type=flt)
    cube = resid.reshape(groups, extent, extent, extent)
    term_b = jnp.einsum("gabc,gacr->gbr", cube, pair_ac, preferred_element_type=flt)
    term_c = jnp.einsum("gabc,gabr->gcr", cube, pair_ab, preferred_element_type=flt)
    return (resid, term_a, term_b, term_c)


def spread(index, terms, count):
    onehot = (index[:, None] == jnp.arange(count, dtype=jnp.int32)[None, :]).astype(jnp.float32)
    return jnp.einsum("gs,gar->sar", onehot, terms, precision=lax.Precision.HIGHEST)


def on_device(factor_a, factor_b, factor_c, observed, coords, counts):
    extent = observed.shape[4]
    columns = factor_a.shape[2]
    slots = observed.shape[3]
    slab_first = lax.all_gather(factor_a, ("ja", "ka"), axis=1, tiled=True)[0]
    slab_second = lax.all_gather(factor_b, ("ia", "ka"), axis=1, tiled=True)[0]
    slab_third = lax.all_gather(factor_c, ("ia", "ja"), axis=1, tiled=True)[0]
    tiles_first = slab_first.reshape(-1, extent, columns)
    tiles_second = slab_second.reshape(-1, extent, columns)
    tiles_third = slab_third.reshape(-1, extent, columns)
    count_first = tiles_first.shape[0]
    count_second = tiles_second.shape[0]
    count_third = tiles_third.shape[0]
    per_turn = 4
    turns = slots // per_turn
    blocks = observed[0, 0, 0].reshape(turns, per_turn, extent, extent * extent)
    places = coords[:, 0, 0, 0, :].reshape(3, turns, per_turn)
    weights = (
        (jnp.arange(slots, dtype=jnp.int32) < counts[0, 0, 0])
        .astype(jnp.float32)
        .reshape(turns, per_turn)
    )

    def turn_step(carry, inputs):
        acc_first, acc_second, acc_third = carry
        data_blocks, where_first, where_second, where_third, weight = inputs
        resid, term_a, term_b, term_c = block_terms(
            tiles_first[where_first],
            tiles_second[where_second],
            tiles_third[where_third],
            data_blocks,
            weight,
        )
        acc_first = acc_first + spread(where_first, term_a, count_first)
        acc_second = acc_second + spread(where_second, term_b, count_second)
        acc_third = acc_third + spread(where_third, term_c, count_third)
        return ((acc_first, acc_second, acc_third), resid)

    init = (
        jnp.zeros((count_first, extent, columns), jnp.float32),
        jnp.zeros((count_second, extent, columns), jnp.float32),
        jnp.zeros((count_third, extent, columns), jnp.float32),
    )
    (acc_first, acc_second, acc_third), resids = lax.scan(
        turn_step, init, (blocks, places[0], places[1], places[2], weights)
    )
    residual = resids.reshape(1, 1, 1, slots, extent, extent * extent)
    scale = 1.0 / extent
    grad_a = lax.psum_scatter(
        (acc_first * scale).reshape(1, -1, columns), ("ja", "ka"), scatter_dimension=1, tiled=True
    )
    grad_b = lax.psum_scatter(
        (acc_second * scale).reshape(1, -1, columns).astype(jnp.bfloat16),
        ("ia", "ka"),
        scatter_dimension=1,
        tiled=True,
    ).astype(jnp.float32)
    third_terms = (acc_third * scale).reshape(1, -1, columns)
    grad_c = lax.psum_scatter(third_terms, ("ia", "ja"), scatter_dimension=1, tiled=True)
    return (residual, grad_a, grad_b, grad_c)


def solution(mesh):
    return jax.shard_map(
        on_device,
        mesh=mesh,
        in_specs=(
            P("ia", ("ja", "ka"), None),
            P("ja", ("ia", "ka"), None),
            P("ka", ("ia", "ja"), None),
            P("ia", "ja", "ka", None, None, None),
            P(None, "ia", "ja", "ka", None),
            P("ia", "ja", "ka"),
        ),
        out_specs=(
            P("ia", "ja", "ka", None, None, None),
            P("ia", ("ja", "ka"), None),
            P("ja", ("ia", "ka"), None),
            P("ka", ("ia", "ja"), None),
        ),
        check_vma=False,
    )
```

profile of v0, /device:TPU:38, one launch (start us, length us, event | category | flops | bytes accessed | tf_op | source)
XLA Modules:
  0.0 1859.3 jit_solution(7790301085948649868)
XLA Ops:
  9.6 55.7 %all_gather.10 = bf16[1,1024,128]{2,1,0:T(8,128)(2,1)S(1)} all-gather(bf16[1,32,128]{2,1,0:T(8,128)(2,1)} %param.9), channel_id=1, replica_groups=mesh['ia'=8,'ja'=16,'ka'=4] {'ia','ka'}, dimensions={1}, use_global_device_ids=true | all-gather | bytes 270336 | tf_op jit(solution)/shard_map/all_gather | solution.py:34
  65.3 220.2 %all_gather.9 = bf16[1,2048,128]{2,1,0:T(8,128)(2,1)} all-gather(bf16[1,32,128]{2,1,0:T(8,128)(2,1)} %param.8), channel_id=1, replica_groups=mesh['ia'=8,'ja'=16,'ka'=4] {'ja','ka'}, dimensions={1}, use_global_device_ids=true | all-gather | bytes 532480 | tf_op jit(solution)/shard_map/all_gather | solution.py:33
  285.5 87.3 %all-gather.2.cloned.1.call-done = bf16[1,4096,128]{2,1,0:T(8,128)(2,1)} async-done(((bf16[1,32,128]{2,1,0:T(8,128)(2,1)}), bf16[1,4096,128]{2,1,0:T(8,128)(2,1)}) %all-gather.2.cloned.1.call-update) | async-done | bytes 1048592 | tf_op jit(solution)/shard_map/all_gather | solution.py:35
  372.7 141.4 %while.17 = (s32[]{:T(128)}, f32[64,32,128]{2,0,1:T(8,128)S(1)}, f32[32,32,128]{2,0,1:T(8,128)}, f32[128,32,128]{2,0,1:T(8,128)S(1)}, bf16[9,4,32,1024]{3,2,1,0:...) while((s32[]{:T(128)}, f32[64,32,128]{2,0,1:T(8,128)S(1)}, ...), condition=%wide.region_1.2_spmd.clone, body=%wide.region_0.1_spmd.clone.sunk | while | flops 182194080 | bytes 19707744 | solution.py:72
  373.4 1.6 gather_fusion
  375.6 1.8 gather_fusion.1
  377.5 2.1 bitcast_dynamic-update-slice_fusion.2
  380.9 1.8 reshape.218
  382.7 1.7 fusion.81
  384.4 1.8 fusion.80
  389.1 1.6 gather_fusion
  391.3 1.8 gather_fusion.1
  393.2 2.1 bitcast_dynamic-update-slice_fusion.2
  396.6 1.8 reshape.218
  398.4 1.7 fusion.81
  400.1 1.7 fusion.80
  402.6 1.6 select_add_fusion.2
  404.9 1.6 gather_fusion
  407.0 1.8 gather_fusion.1
  408.9 2.1 bitcast_dynamic-update-slice_fusion.2
  412.3 1.8 reshape.218
  414.1 1.7 fusion.81
  415.8 1.8 fusion.80
  420.6 1.6 gather_fusion
  422.7 1.8 gather_fusion.1
  424.6 2.1 bitcast_dynamic-update-slice_fusion.2
  428.0 1.8 reshape.218
  429.8 1.7 fusion.81
  431.6 1.8 fusion.80
  436.3 1.6 gather_fusion
  438.4 1.8 gather_fusion.1
  440.3 2.1 bitcast_dynamic-update-slice_fusion.2
  443.7 1.8 reshape.218
  445.5 1.7 fusion.81
  447.3 1.8 fusion.80
  452.0 1.6 gather_fusion
  454.2 1.8 gather_fusion.1
  456.0 2.1 bitcast_dynamic-update-slice_fusion.2
  459.5 1.8 reshape.218
  461.3 1.7 fusion.81
  463.0 1.8 fusion.80
  467.7 1.6 gather_fusion
  469.9 1.8 gather_fusion.1
  471.8 2.1 bitcast_dynamic-update-slice_fusion.2
  475.2 1.8 reshape.218
  477.0 1.7 fusion.81
  478.7 1.8 fusion.80
  483.4 1.6 gather_fusion
  485.6 1.8 gather_fusion.1
  487.5 2.1 bitcast_dynamic-update-slice_fusion.2
  490.9 1.8 reshape.218
  492.7 1.7 fusion.81
  494.4 1.8 fusion.80
  499.1 1.6 gather_fusion
  501.3 1.8 gather_fusion.1
  503.2 2.1 bitcast_dynamic-update-slice_fusion.2
  506.6 1.8 reshape.218
  508.4 1.7 fusion.81
  510.1 1.8 fusion.80
  516.2 1.6 copy.13
  518.1 2.6 copy.15
  520.7 124.0 %reduce-scatter.6.cloned.1.call-done = bf16[1,32,128]{2,1,0:T(8,128)(2,1)} async-done(((bf16[1,1024,128]{2,1,0:T(8,128)(2,1)}), bf16[1,32,128]{2,1,0:T(8,128)(2,1)}) %reduce-scatter.6.cloned.1.call-update) | async-done | bytes 8208 | tf_op jit(solution)/shard_map/reduce_scatter | solution.py:80
  645.9 448.9 %reduce-scatter.4.cloned.1.call-done = f32[1,32,128]{2,1,0:T(8,128)} async-done(((f32[1,2048,128]{2,1,0:T(8,128)}), f32[1,32,128]{2,1,0:T(8,128)}) %reduce-scatter.4.cloned.1.call-update) | async-done | bytes 16400 | tf_op jit(solution)/shard_map/reduce_scatter | solution.py:77
  1094.8 758.0 %reduce-scatter.8.cloned.1.call-done = f32[1,32,128]{2,1,0:T(8,128)} async-done(((f32[1,4096,128]{2,1,0:T(8,128)}), f32[1,32,128]{2,1,0:T(8,128)}) %reduce-scatter.8.cloned.1.call-update) | async-done | bytes 16400 | tf_op jit(solution)/shard_map/reduce_scatter | solution.py:87
  (255 shorter events, 46.4 us)
Async XLA Ops:
  7.2 365.6 %all-gather.2.cloned.1.call-start = ((), (), s32[]{:S(2)}) async-start(), calls=%async_computation.3 | async-start | bytes 1056768 | tf_op jit(solution)/shard_map/all_gather | solution.py:35
  7.9 636.7 %reduce-scatter.6.cloned.1.call-start = ((), (), s32[]{:S(2)}) async-start(), calls=%async_computation.5 | async-start | bytes 270336 | tf_op jit(solution)/shard_map/reduce_scatter | solution.py:80
  372.7 0.6 copy-start.4
  372.7 4.7 copy-start.2
  382.7 3.5 copy-start
  386.8 1.6 copy-start.1
  386.8 1.6 copy-start.3
  386.8 1.6 copy-start.5
  388.5 0.6 copy-start.4
  388.5 4.7 copy-start.2
  398.4 3.5 copy-start
  402.5 1.6 copy-start.1
  402.5 1.6 copy-start.3
  402.5 1.6 copy-start.5
  404.2 0.6 copy-start.4
  404.2 4.7 copy-start.2
  414.1 3.5 copy-start
  418.2 1.6 copy-start.1
  418.3 1.6 copy-start.3
  418.3 1.6 copy-start.5
  419.9 0.6 copy-start.4
  419.9 4.7 copy-start.2
  429.8 3.5 copy-start
  434.0 1.6 copy-start.1
  434.0 1.6 copy-start.3
  434.0 1.6 copy-start.5
  435.6 0.6 copy-start.4
  435.6 4.7 copy-start.2
  445.5 3.5 copy-start
  449.7 1.6 copy-start.1
  449.7 1.6 copy-start.3
  449.7 1.6 copy-start.5
  451.3 0.6 copy-start.4
  451.3 4.7 copy-start.2
  461.3 3.5 copy-start
  465.4 1.6 copy-start.1
  465.4 1.6 copy-start.3
  465.4 1.6 copy-start.5
  467.0 0.6 copy-start.4
  467.0 4.7 copy-start.2
  477.0 3.5 copy-start
  481.1 1.6 copy-start.1
  481.1 1.6 copy-start.3
  481.1 1.6 copy-start.5
  482.7 0.6 copy-start.4
  482.8 4.7 copy-start.2
  492.7 3.5 copy-start
  496.8 1.6 copy-start.1
  496.8 1.6 copy-start.3
  496.8 1.6 copy-start.5
  498.5 0.6 copy-start.4
  498.5 4.7 copy-start.2
  508.4 3.5 copy-start
  512.5 1.6 copy-start.1
  512.5 1.6 copy-start.3
  512.5 1.6 copy-start.5
  516.1 578.7 %reduce-scatter.4.cloned.1.call-start = ((), (), s32[]{:S(2)}) async-start(), calls=%async_computation.4 | async-start | bytes 1064960 | tf_op jit(solution)/shard_map/reduce_scatter | solution.py:77
  517.8 1334.9 %reduce-scatter.8.cloned.1.call-start = ((), (), s32[]{:S(2)}) async-start(), calls=%async_computation.6 | async-start | bytes 2113536 | tf_op jit(solution)/shard_map/reduce_scatter | solution.py:87
Sparse Core Ops, SparseCore 0:
  10.1 362.5 all-gather.1
  516.2 128.3 reduce-scatter.5
  648.2 446.5 reduce-scatter.3
  1098.0 754.6 reduce-scatter.7
where the time goes:
time: 1860 us
  waiting for transfers between devices  1420 us (76%)
  blocking collectives  276 us (15%)
  matrix products  81.6 us (4%)
  local copies, waits for them, and re-layouts  62.9 us (3%)
    reduce_scatter x1, waiting for transfers between devices, on_device(): lax.psum_scatter(third_terms, ('ia', 'ja'), scatter_dimension=1, tiled=True)  758 us
    reduce_scatter x1, waiting for transfers between devices, on_device(): lax.psum_scatter((acc_first * scale).reshape(1, -1, columns), ('ja', 'ka'...  449 us
    all_gather x1, blocking collectives, on_device(): slab_first = lax.all_gather(factor_a, ('ja', 'ka'), axis=1, tiled=True)[0]  220 us
    reduce_scatter x1, waiting for transfers between devices, on_device(): lax.psum_scatter((acc_second * scale).reshape(1, -1, columns).astype(jnp....  124 us
    all_gather x1, waiting for transfers between devices, on_device(): slab_third = lax.all_gather(factor_c, ('ia', 'ja'), axis=1, tiled=True)[0]  87.3 us
    all_gather x1, blocking collectives, on_device(): slab_second = lax.all_gather(factor_b, ('ia', 'ka'), axis=1, tiled=True)[0]  55.7 us
  transfers between devices with their start and end apart: 4, of which 4 were waited for; matrix products, arithmetic and copies ran while one was open for 0% of the time, Pallas kernels for 0%

commit v1 on v0

v1 whole, which is shorter than its diff:
```python
import jax
import jax.numpy as jnp
from jax import lax
from jax.experimental import pallas as pl
from jax.experimental.pallas import tpu as pltpu
from jax.sharding import Mesh, PartitionSpec as P

BF = jnp.bfloat16
F32 = jnp.float32
T = 32
R = 128
UNROLL = 4

AB = 768
CY = 640


def cp_kernel(off, ab, c_own, c_oth, obs, res, out_ab, out_own, out_oth, acc_ab, acc_c):
    slots = obs.shape[0]
    acc_ab[...] = jnp.zeros_like(acc_ab)
    acc_c[...] = jnp.zeros_like(acc_c)
    count = off[5, 0]

    def at(row, s):
        return pl.ds(pl.multiple_of(off[row, s], T), T)

    def terms(s):
        ta = ab[at(0, s), :]
        tb = ab[at(1, s), :].astype(F32)
        where_c = at(2, s)
        tc = jnp.where(off[4, s] == 0, c_own[where_c, :].astype(F32), c_oth[where_c, :].astype(F32))
        pair = (tb[:, None, :] * tc[None, :, :]).reshape(T * T, R).astype(BF)
        model = lax.dot_general(ta, pair, (((1,), (1,)), ((), ())), preferred_element_type=F32)
        live = (s < count).astype(F32)
        resid = (live * (model - obs[s].astype(F32))).astype(BF)
        res[s] = resid
        term_a = jnp.dot(resid, pair, preferred_element_type=F32)
        wide = lax.dot_general(resid, ta, (((0,), (0,)), ((), ())), preferred_element_type=F32)
        wide = wide.reshape(T, T, R)
        term_b = jnp.sum(wide * tc[None, :, :], axis=1)
        term_c = jnp.sum(wide * tb[:, None, :], axis=0)
        return term_a, term_b, term_c

    def group(g, carry):
        base = g * UNROLL

        @pl.when(base < count)
        def _():
            found = [terms(base + u) for u in range(UNROLL)]
            for u, (term_a, term_b, term_c) in enumerate(found):
                s = base + u
                acc_ab[at(0, s), :] += term_a
                acc_ab[at(1, s), :] += term_b
                acc_c[at(3, s), :] += term_c

        @pl.when(base >= count)
        def _():
            res[pl.ds(base, UNROLL)] = jnp.zeros((UNROLL,) + res.shape[1:], BF)

        return carry

    lax.fori_loop(0, slots // UNROLL, group, 0)
    scale = 1.0 / T
    half = out_own.shape[0]
    out_ab[...] = (acc_ab[...] * scale).astype(BF)
    out_own[...] = acc_c[:half, :] * scale
    out_oth[...] = (acc_c[half:, :] * scale).astype(BF)


def run_kernel(off, ab, c_own, c_oth, obs):
    slots = obs.shape[0]
    vmem = pl.BlockSpec(memory_space=pltpu.VMEM)
    half = 4 * 512
    return pl.pallas_call(
        cp_kernel,
        out_shape=(
            jax.ShapeDtypeStruct((slots, T, T * T), BF),
            jax.ShapeDtypeStruct((4 * AB, R), BF),
            jax.ShapeDtypeStruct((half, R), F32),
            jax.ShapeDtypeStruct((half, R), BF),
        ),
        in_specs=[pl.BlockSpec(memory_space=pltpu.SMEM), vmem, vmem, vmem, vmem],
        out_specs=(vmem, vmem, vmem, vmem),
        scratch_shapes=[pltpu.VMEM((4 * AB, R), F32), pltpu.VMEM((2 * half, R), F32)],
        compiler_params=pltpu.CompilerParams(vmem_limit_bytes=40 * 1024 * 1024),
        cost_estimate=pl.CostEstimate(
            flops=slots * 8 * T * T * T * R, bytes_accessed=12_000_000, transcendentals=0
        ),
    )(off, ab, c_own, c_oth, obs)


def on_device(factor_a, factor_b, factor_c, observed, coords, counts):
    slots = observed.shape[3]
    fa, fb, fc = factor_a[0], factor_b[0], factor_c[0]
    zl, co, zh = lax.axis_index("zl"), lax.axis_index("co"), lax.axis_index("zh")
    same_zl = (jnp.arange(4) == zl)[:, None, None]
    swap = [(0, 1), (1, 0)]

    pa, pb, pc = coords[0].reshape(slots), coords[1].reshape(slots), coords[2].reshape(slots)
    off_a = (pa % 4) * AB + (pa // 4 % 4) * 128 + (pa // 16) * T
    off_b = (pb % 4) * AB + 512 + ((pb // 4 % 2) ^ co) * 128 + (pb // 8) * T
    c_y, c_zh, c_rel, c_zl = pc % 4, pc // 4 % 4, (pc // 16 % 2) ^ co, pc // 32
    in_plane = (c_zl * 4 + c_zh) * T
    off_c = c_y * CY + in_plane
    off_acc = c_rel * 2048 + c_y * 512 + in_plane
    live = jnp.broadcast_to(counts.reshape(1), (slots,))
    off = jnp.stack([off_a, off_b, off_c, off_acc, c_rel, live]).astype(jnp.int32)

    second = jnp.where(same_zl[:, :, :, None], fa, fb)
    send = jnp.concatenate(
        [jnp.broadcast_to(fc, (4, 4, T, R)), jnp.broadcast_to(second, (4, 4, T, R))], axis=2
    )
    got = lax.all_to_all(send.reshape(16, 2 * T, R), ("zl", "zh"), 0, 0, tiled=True)
    got = got.reshape(4, 4, 2 * T, R)
    c_z = got[:, :, :T].reshape(16 * T, R)
    a_z = lax.dynamic_index_in_dim(got, zl, 0, keepdims=False)[:, T:].reshape(4 * T, R)
    b_z = lax.dynamic_index_in_dim(got, zh, 1, keepdims=False)[:, T:]
    b_z = jnp.where(same_zl, fb, b_z).reshape(4 * T, R)
    b_oth = lax.ppermute(b_z, "co", swap)
    by_y = lax.all_gather(jnp.concatenate([c_z, a_z]), "y", axis=0)
    c_oth = lax.ppermute(by_y, "co", swap)
    by_x = lax.all_gather(
        jnp.concatenate([by_y[:, 512:].reshape(512, R), b_z, b_oth]), "x", axis=0
    )

    res, sum_ab, sum_own, sum_oth = run_kernel(
        off,
        by_x.reshape(4 * AB, R),
        by_y.reshape(4 * CY, R),
        c_oth.reshape(4 * CY, R),
        observed[0, 0, 0],
    )

    c_in = lax.ppermute(sum_oth, "co", swap)
    ab_in = lax.all_to_all(sum_ab.reshape(4, AB, R), "x", 0, 0, tiled=True)
    ab = jnp.sum(ab_in.astype(F32), axis=0)
    c_sum = (sum_own + c_in.astype(F32)).astype(BF).reshape(4, 512, R)
    b_in = lax.ppermute(ab[640:].astype(BF), "co", swap)
    ca_in = lax.all_to_all(
        jnp.concatenate([c_sum, ab[:512].astype(BF).reshape(4, 128, R)], axis=1),
        "y", 0, 0, tiled=True,
    )
    ca = jnp.sum(ca_in.astype(F32), axis=0)
    b_sum = (ab[512:640] + b_in.astype(F32)).reshape(4, 1, T, R)
    a_sum = ca[512:].reshape(1, 4, T, R)
    second = jnp.where(same_zl[:, :, :, None], a_sum, b_sum).astype(BF)
    send = jnp.concatenate([ca[:512].astype(BF).reshape(4, 4, T, R), second], axis=2)
    got = lax.all_to_all(send.reshape(16, 2 * T, R), ("zl", "zh"), 0, 0, tiled=True)
    got = got.reshape(4, 4, 2 * T, R)
    grad_c = jnp.sum(got[:, :, :T].astype(F32), axis=(0, 1))
    grad_a = jnp.sum(
        lax.dynamic_index_in_dim(got, zl, 0, keepdims=False)[:, T:].astype(F32), axis=0
    )
    b_got = lax.dynamic_index_in_dim(got, zh, 1, keepdims=False)[:, T:].astype(F32)
    grad_b = jnp.sum(jnp.where(same_zl, b_sum[:, 0], b_got), axis=0)
    return (res.reshape(observed.shape), grad_a[None], grad_b[None], grad_c[None])


def solution(mesh):
    fine = Mesh(mesh.devices.reshape(4, 2, 4, 4, 4), ("zl", "co", "zh", "y", "x"))
    ia, ja = ("zl", "co"), ("zh", "y")
    return jax.shard_map(
        on_device,
        mesh=fine,
        in_specs=(
            P(ia, (*ja, "x"), None),
            P(ja, (*ia, "x"), None),
            P("x", (*ia, *ja), None),
            P(ia, ja, "x", None, None, None),
            P(None, ia, ja, "x", None),
            P(ia, ja, "x"),
        ),
        out_specs=(
            P(ia, ja, "x", None, None, None),
            P(ia, (*ja, "x"), None),
            P(ja, (*ia, "x"), None),
            P("x", (*ia, *ja), None),
        ),
        check_vma=False,
    )
```

time: 1860 us -> 147 us (0.08)
  the two profiles are of different devices: /device:TPU:38 before, /device:TPU:64 now
where the time goes in v1:
time: 147 us
  blocking collectives  51.7 us (35%)
  waiting for transfers between devices  41.2 us (28%)
  starting transfers between devices  34.1 us (23%)
  Pallas kernels  10.8 us (7%)
  other arithmetic  4.95 us (3%)
  local copies, waits for them, and re-layouts  2.69 us (2%)
  between operations  1.49 us (1%)
    all_to_all x1, blocking collectives, on_device(): lax.all_to_all(send.reshape(16, 2 * T, R), ('zl', 'zh'), 0, 0, tiled=True)  23.2 us
    all_to_all x1, waiting for transfers between devices, on_device(): lax.all_to_all(send.reshape(16, 2 * T, R), ('zl', 'zh'), 0, 0, tiled=True)  19.9 us
    all_to_all x1, starting transfers between devices, on_device(): lax.all_to_all(send.reshape(16, 2 * T, R), ('zl', 'zh'), 0, 0, tiled=True)  14.8 us
    all_gather x1, blocking collectives, on_device(): by_y = lax.all_gather(jnp.concatenate([c_z, a_z]), 'y', axis=0)  14.3 us
    all_gather x1, blocking collectives, on_device(): lax.all_gather(jnp.concatenate([by_y[:, 512:].reshape(512, R), b_z, b_oth...  14.1 us
    all_to_all x1, waiting for transfers between devices, on_device(): ab_in = lax.all_to_all(sum_ab.reshape(4, AB, R), 'x', 0, 0, tiled=True)  12.8 us
    pallas_call x1, Pallas kernels, run_kernel(): pl.pallas_call(cp_kernel, out_shape=(jax.ShapeDtypeStruct((slots, T, T *...  10.8 us
    all_to_all x1, waiting for transfers between devices, on_device(): lax.all_to_all(jnp.concatenate([c_sum, ab[:512].astype(BF).reshape(4, 128...  7.34 us
  transfers between devices with their start and end apart: 7, of which 5 were waited for; matrix products, arithmetic and copies ran while one was open for 0% of the time, Pallas kernels for 0%

profile of v1, /device:TPU:64, one launch (start us, length us, event | category | flops | bytes accessed | tf_op | source)
XLA Modules:
  0.0 146.8 jit_solution(16385243754799990206)
XLA Ops:
  0.6 0.0 copy-start.2
  0.7 0.8 broadcast_select_fusion
  1.5 0.7 broadcast_in_dim.84
  2.2 0.0 copy-start.1
  2.2 0.7 pad_maximum_fusion.1
  2.9 14.8 %all-to-all-start = ((bf16[16,64,128]{2,1,0:T(8,128)(2,1)}), bf16[16,64,128]{2,1,0:T(8,128)(2,1)S(1)}, u32[]{:S(2)}, u32[]{:S(2)}) async-start(bf16[16,64,128]{2,1,0:T(8,128)(2,1)} %bitcast.7), calls=%async_computation | async-start | bytes 524288 | tf_op jit(solution)/shard_map/all_to_all | solution.py:113
  17.7 0.0 copy-done.2
  17.7 19.9 %all-to-all-done = bf16[16,64,128]{2,1,0:T(8,128)(2,1)S(1)} async-done(((bf16[16,64,128]{2,1,0:T(8,128)(2,1)}), bf16[16,64,128]{2,1,0:T(8,128)(2,1)S(1)}, u32[]{:S(2)}, u32[]{:S(2)}) %all-to-all-start) | async-done | bytes 262176 | tf_op jit(solution)/shard_map/all_to_all | solution.py:113
  37.7 14.3 %all-gather.c_own = bf16[2560,128]{1,0:T(8,128)(2,1)S(1)} all-gather(bf16[640,128]{1,0:T(8,128)(2,1)S(1)} %pad_maximum_fusion.4), channel_id=2, replica_groups=mesh['zl'=4,'co'=2,'zh'=4,'y'=4,'x'=4] {'y'}, dimensions={0}, use_global_device_ids=true | all-gather | bytes 819200 | tf_op jit(solution)/shard_map/all_gather | solution.py:120
  52.1 1.9 %collective-permute-start.1 = (bf16[4,640,128]{2,1,0:T(8,128)(2,1)S(1)}, bf16[4,640,128]{2,1,0:T(8,128)(2,1)S(1)}, u32[]{:S(2)}, u32[]{:S(2)}) collective-permute-start(bf16[4,640,128]{2,1,0:T(8,128)(2,1)S(1)} %bitcast.98), channel_id=1, source_target_pairs={{0,64},{64,0},{1,65},{65,1},{2,66},{66,2},{3,67},{67,3},{4,68},{68... | collective-permute-start | bytes 1966088 | tf_op jit(solution)/shard_map/ppermute | solution.py:121
  54.0 0.0 copy-done.1
  54.0 0.1 slice_select_fusion
  54.1 2.4 %collective-permute-start = (bf16[128,128]{1,0:T(8,128)(2,1)S(1)}, bf16[128,128]{1,0:T(8,128)(2,1)S(1)}, u32[]{:S(2)}, u32[]{:S(2)}) collective-permute-start(bf16[128,128]{1,0:T(8,128)(2,1)S(1)} %bitcast.115), channel_id=1, source_target_pairs={{0,64},{64,0},{1,65},{65,1},{2,66},{66,2},{3,67},{67,3},{4,68},{68... | collective-permute-start | bytes 98312 | tf_op jit(solution)/shard_map/ppermute | solution.py:119
  57.2 0.1 collective-permute-done
  57.3 14.1 %all-gather.1.ab = bf16[3072,128]{1,0:T(8,128)(2,1)S(1)} all-gather(bf16[768,128]{1,0:T(8,128)(2,1)S(1)} %pad_maximum_fusion.3), channel_id=3, replica_groups=mesh['zl'=4,'co'=2,'zh'=4,'y'=4,'x'=4] {'x'}, dimensions={0}, use_global_device_ids=true | all-gather | bytes 983040 | tf_op jit(solution)/shard_map/all_gather | solution.py:122
  71.4 0.0 collective-permute-done.1
  71.4 0.0 copy-start
  71.4 1.7 %copy-done = bf16[1,1,1,36,32,1024]{5,4,3,2,1,0:T(8,128)(2,1)S(1)} copy-done((bf16[1,1,1,36,32,1024]{5,4,3,2,1,0:T(8,128)(2,1)S(1)}, bf16[1,1,1,36,32,1024]{5,4,3,2,1,0:T(8,128)(2,1)}, u32[]{:S(2)}) %copy-start) | copy-done | bytes 2359320
  73.1 10.8 %shard_map.93 = (bf16[36,32,1024]{2,1,0:T(8,128)(2,1)}, bf16[3072,128]{1,0:T(8,128)(2,1)}, f32[2048,128]{1,0:T(8,128)S(1)}, bf16[2048,128]{1,0:T(8,128)(2,1)S(1)}) custom-call(s32[6,36]{1,0:T(8,128)S(1)} %stack.2.off, bf16[3072,128]{1,0:T(8,128)(2,1)S(1)} %all-gather.1.ab, bf16[2560,128]{1,0:T(8,128)(2,1)S(1)} %all-gather.c_own, ...), custom_call_target="tpu_custom_call" | custom-call | flops 1207959552 | bytes 12000000 | tf_op jit(solution)/shard_map/pallas_call | solution.py:74
  83.8 1.9 %collective-permute-start.2 = (bf16[2048,128]{1,0:T(8,128)(2,1)S(1)}, bf16[2048,128]{1,0:T(8,128)(2,1)S(1)}, u32[]{:S(2)}, u32[]{:S(2)}) collective-permute-start(bf16[2048,128]{1,0:T(8,128)(2,1)S(1)} %get-tuple-element.10), channel_id=1, source_target_pairs={{0,64},{64,0},{1,65},{65,1},{2,66},{66,2},{3,67},{67,3},{4,68},{68... | collective-permute-start | bytes 1572872 | tf_op jit(solution)/shard_map/ppermute | solution.py:134
  85.8 7.0 %all-to-all-start.1 = ((bf16[4,768,128]{2,1,0:T(8,128)(2,1)}), bf16[4,768,128]{2,1,0:T(8,128)(2,1)S(1)}, u32[]{:S(2)}, u32[]{:S(2)}) async-start(bf16[4,768,128]{2,1,0:T(8,128)(2,1)} %bitcast.20), calls=%async_computation.1 | async-start | bytes 1572864 | tf_op jit(solution)/shard_map/all_to_all | solution.py:135
  92.8 0.0 collective-permute-done.2
  92.8 0.1 add_convert_fusion
  92.9 12.8 %all-to-all-done.1 = bf16[4,768,128]{2,1,0:T(8,128)(2,1)S(1)} async-done(((bf16[4,768,128]{2,1,0:T(8,128)(2,1)}), bf16[4,768,128]{2,1,0:T(8,128)(2,1)S(1)}, u32[]{:S(2)}, u32[]{:S(2)}) %all-to-all-start.1) | async-done | bytes 786464 | tf_op jit(solution)/shard_map/all_to_all | solution.py:135
  105.7 0.1 convert_reduce_fusion
  105.9 0.9 pad_maximum_fusion
  106.8 4.2 %all-to-all-start.2 = ((bf16[4,640,128]{2,1,0:T(8,128)(2,1)}), bf16[4,640,128]{2,1,0:T(8,128)(2,1)S(1)}, u32[]{:S(2)}, u32[]{:S(2)}) async-start(bf16[4,640,128]{2,1,0:T(8,128)(2,1)} %pad_maximum_fusion), calls=%async_computation.2 | async-start | bytes 1310720 | tf_op jit(solution)/shard_map/all_to_all | solution.py:139
  111.0 1.9 %collective-permute-start.3 = (bf16[128,128]{1,0:T(8,128)(2,1)S(1)}, bf16[128,128]{1,0:T(8,128)(2,1)S(1)}, u32[]{:S(2)}, u32[]{:S(2)}) collective-permute-start(bf16[128,128]{1,0:T(8,128)(2,1)S(1)} %slice.71), channel_id=1, source_target_pairs={{0,64},{64,0},{1,65},{65,1},{2,66},{66,2},{3,67},{67,3},{4,68},{68... | collective-permute-start | bytes 98312 | tf_op jit(solution)/shard_map/ppermute | solution.py:138
  112.9 0.1 broadcast_in_dim.89
  113.0 0.1 broadcast_in_dim.90
  113.0 1.0 collective-permute-done.3
  114.1 7.3 %all-to-all-done.2 = bf16[4,640,128]{2,1,0:T(8,128)(2,1)S(1)} async-done(((bf16[4,640,128]{2,1,0:T(8,128)(2,1)}), bf16[4,640,128]{2,1,0:T(8,128)(2,1)S(1)}, u32[]{:S(2)}, u32[]{:S(2)}) %all-to-all-start.2) | async-done | bytes 655392 | tf_op jit(solution)/shard_map/all_to_all | solution.py:139
  121.4 0.1 convert_reduce_fusion.1
  121.5 0.1 fusion
  121.6 23.2 %all_to_all.20 = bf16[16,64,128]{2,1,0:T(8,128)(2,1)S(1)} all-to-all(bf16[16,64,128]{2,1,0:T(8,128)(2,1)S(1)} %pad_maximum_fusion.2), channel_id=1, replica_groups=mesh['zl'=4,'co'=2,'zh'=4,'y'=4,'x'=4] {'zl','zh'}, dimensions={0} | all-to-all | bytes 524288 | tf_op jit(solution)/shard_map/all_to_all | solution.py:148
  144.9 0.6 convert_reduce_fusion.2
  145.5 0.7 select_reduce_fusion
  146.2 0.6 convert_reduce_fusion.3
  (22 shorter events, 0.3 us)
Async XLA Ops:
  0.6 17.1 %copy-start.2 = (s32[3,1,1,1,36]{4,3,2,1,0:T(1,128)S(1)}, s32[3,1,1,1,36]{4,3,2,1,0:T(1,128)}, u32[]{:S(2)}) copy-start(s32[3,1,1,1,36]{4,3,2,1,0:T(1,128)} %param.10) | copy-start | bytes 1300
  2.2 51.8 %copy-start.1 = (bf16[1,32,128]{2,1,0:T(8,128)(2,1)S(1)}, bf16[1,32,128]{2,1,0:T(8,128)(2,1)}, u32[]{:S(2)}) copy-start(bf16[1,32,128]{2,1,0:T(8,128)(2,1)} %param.7) | copy-start | bytes 24580
  2.9 34.7 %all-to-all-start = ((bf16[16,64,128]{2,1,0:T(8,128)(2,1)}), bf16[16,64,128]{2,1,0:T(8,128)(2,1)S(1)}, u32[]{:S(2)}, u32[]{:S(2)}) async-start(bf16[16,64,128]{2,1,0:T(8,128)(2,1)} %bitcast.7), calls=%async_computation | async-start | bytes 524288 | tf_op jit(solution)/shard_map/all_to_all | solution.py:113
  52.1 19.4 %collective-permute-start.1 = (bf16[4,640,128]{2,1,0:T(8,128)(2,1)S(1)}, bf16[4,640,128]{2,1,0:T(8,128)(2,1)S(1)}, u32[]{:S(2)}, u32[]{:S(2)}) collective-permute-start(bf16[4,640,128]{2,1,0:T(8,128)(2,1)S(1)} %bitcast.98), channel_id=1, source_target_pairs={{0,64},{64,0},{1,65},{65,1},{2,66},{66,2},{3,67},{67,3},{4,68},{68... | collective-permute-start | bytes 1966088 | tf_op jit(solution)/shard_map/ppermute | solution.py:121
  54.1 3.2 %collective-permute-start = (bf16[128,128]{1,0:T(8,128)(2,1)S(1)}, bf16[128,128]{1,0:T(8,128)(2,1)S(1)}, u32[]{:S(2)}, u32[]{:S(2)}) collective-permute-start(bf16[128,128]{1,0:T(8,128)(2,1)S(1)} %bitcast.115), channel_id=1, source_target_pairs={{0,64},{64,0},{1,65},{65,1},{2,66},{66,2},{3,67},{67,3},{4,68},{68... | collective-permute-start | bytes 98312 | tf_op jit(solution)/shard_map/ppermute | solution.py:119
  71.4 1.7 %copy-start = (bf16[1,1,1,36,32,1024]{5,4,3,2,1,0:T(8,128)(2,1)S(1)}, bf16[1,1,1,36,32,1024]{5,4,3,2,1,0:T(8,128)(2,1)}, u32[]{:S(2)}) copy-start(bf16[1,1,1,36,32,1024]{5,4,3,2,1,0:T(8,128)(2,1)} %param.9) | copy-start | bytes 7077892
  83.8 8.9 %collective-permute-start.2 = (bf16[2048,128]{1,0:T(8,128)(2,1)S(1)}, bf16[2048,128]{1,0:T(8,128)(2,1)S(1)}, u32[]{:S(2)}, u32[]{:S(2)}) collective-permute-start(bf16[2048,128]{1,0:T(8,128)(2,1)S(1)} %get-tuple-element.10), channel_id=1, source_target_pairs={{0,64},{64,0},{1,65},{65,1},{2,66},{66,2},{3,67},{67,3},{4,68},{68... | collective-permute-start | bytes 1572872 | tf_op jit(solution)/shard_map/ppermute | solution.py:134
  85.8 20.0 %all-to-all-start.1 = ((bf16[4,768,128]{2,1,0:T(8,128)(2,1)}), bf16[4,768,128]{2,1,0:T(8,128)(2,1)S(1)}, u32[]{:S(2)}, u32[]{:S(2)}) async-start(bf16[4,768,128]{2,1,0:T(8,128)(2,1)} %bitcast.20), calls=%async_computation.1 | async-start | bytes 1572864 | tf_op jit(solution)/shard_map/all_to_all | solution.py:135
  106.8 14.6 %all-to-all-start.2 = ((bf16[4,640,128]{2,1,0:T(8,128)(2,1)}), bf16[4,640,128]{2,1,0:T(8,128)(2,1)S(1)}, u32[]{:S(2)}, u32[]{:S(2)}) async-start(bf16[4,640,128]{2,1,0:T(8,128)(2,1)} %pad_maximum_fusion), calls=%async_computation.2 | async-start | bytes 1310720 | tf_op jit(solution)/shard_map/all_to_all | solution.py:139
  111.0 3.1 %collective-permute-start.3 = (bf16[128,128]{1,0:T(8,128)(2,1)S(1)}, bf16[128,128]{1,0:T(8,128)(2,1)S(1)}, u32[]{:S(2)}, u32[]{:S(2)}) collective-permute-start(bf16[128,128]{1,0:T(8,128)(2,1)S(1)} %slice.71), channel_id=1, source_target_pairs={{0,64},{64,0},{1,65},{65,1},{2,66},{66,2},{3,67},{67,3},{4,68},{68... | collective-permute-start | bytes 98312 | tf_op jit(solution)/shard_map/ppermute | solution.py:138

commit v2 on v1

v2 whole, which is shorter than its diff:
```python
import jax
import jax.numpy as jnp
from jax import lax
from jax.experimental import pallas as pl
from jax.experimental.pallas import tpu as pltpu
from jax.sharding import Mesh, PartitionSpec as P

BF = jnp.bfloat16
F32 = jnp.float32
T = 32
R = 128
UNROLL = 4
VMEM = pl.BlockSpec(memory_space=pltpu.VMEM)
SMEM = pl.BlockSpec(memory_space=pltpu.SMEM)
HBM = pl.BlockSpec(memory_space=pltpu.HBM)

AB = 768
CY = 640


def sds(rows, dtype=BF):
    return jax.ShapeDtypeStruct(rows + (R,) if isinstance(rows, tuple) else (rows, R), dtype)


def small(kernel, out_shape, *args):
    return pl.pallas_call(
        kernel,
        out_shape=out_shape,
        in_specs=[VMEM] * len(args),
        out_specs=jax.tree.map(lambda _: VMEM, out_shape),
        compiler_params=pltpu.CompilerParams(vmem_limit_bytes=8 * 1024 * 1024),
    )(*args)


def spread_kernel(fa, fb, fc, send, b_own, a_v, c_v, sem):
    zl = lax.axis_index("zl")
    copies = [
        pltpu.make_async_copy(src, dst, sem.at[n])
        for n, (src, dst) in enumerate(((fa, a_v), (fb, b_own), (fc, c_v)))
    ]
    for copy in copies:
        copy.start()
    for copy in copies:
        copy.wait()
    for i in range(4):
        second = jnp.where(zl == i, a_v[...], b_own[...])
        for j in range(4):
            send[4 * i + j, :T, :] = c_v[...]
            send[4 * i + j, T:, :] = second


def spread(fa, fb, fc):
    return pl.pallas_call(
        spread_kernel,
        out_shape=(sds((16, 2 * T)), sds(T)),
        in_specs=[HBM, HBM, HBM],
        out_specs=(VMEM, VMEM),
        scratch_shapes=[
            pltpu.VMEM((T, R), BF), pltpu.VMEM((T, R), BF), pltpu.SemaphoreType.DMA((3,))
        ],
        compiler_params=pltpu.CompilerParams(vmem_limit_bytes=60 * 1024 * 1024),
    )(fa, fb, fc)


def split_kernel(got, b_own, y_send, b_z):
    zl, zh = lax.axis_index("zl"), lax.axis_index("zh")
    for m in range(16):
        tile = got[m, :T, :]
        for k in range(4):
            y_send[k, m * T : (m + 1) * T, :] = tile
    for j in range(4):
        tile = got[4 * zl + j, T:, :]
        for k in range(4):
            y_send[k, 512 + j * T : 512 + (j + 1) * T, :] = tile
    for i in range(4):
        b_z[i * T : (i + 1) * T, :] = jnp.where(zl == i, b_own[...], got[4 * i + zh, T:, :])


def join_kernel(by_y, b_z, b_oth, x_send):
    for j in range(4):
        x_send[128 * j : 128 * (j + 1), :] = by_y[j, 512:, :]
    x_send[512:640, :] = b_z[...]
    x_send[640:, :] = b_oth[...]


def total(ref, rows):
    parts = [ref[k, rows, :].astype(F32) for k in range(4)]
    return (parts[0] + parts[1]) + (parts[2] + parts[3])


def pack_y_kernel(ab_in, own, c_in, y_send, b_own, b_oth):
    for k in range(4):
        rows = slice(512 * k, 512 * (k + 1))
        y_send[k, :512, :] = (own[rows, :] + c_in[rows, :].astype(F32)).astype(BF)
        y_send[k, 512:, :] = total(ab_in, slice(128 * k, 128 * (k + 1))).astype(BF)
    b_own[...] = total(ab_in, slice(512, 640))
    b_oth[...] = total(ab_in, slice(640, 768)).astype(BF)


def pack_z_kernel(ca_in, b_own, b_in, send, b_keep):
    zl = lax.axis_index("zl")
    for m in range(16):
        send[m, :T, :] = total(ca_in, slice(m * T, (m + 1) * T)).astype(BF)
    a = [total(ca_in, slice(512 + j * T, 512 + (j + 1) * T)) for j in range(4)]
    for i in range(4):
        rows = slice(i * T, (i + 1) * T)
        b = b_own[rows, :] + b_in[rows, :].astype(F32)
        for j in range(4):
            send[4 * i + j, T:, :] = jnp.where(zl == i, a[j], b).astype(BF)

        @pl.when(zl == i)
        def _():
            b_keep[...] = b


def last_kernel(got, b_keep, grad_a, grad_b, grad_c):
    zl, zh = lax.axis_index("zl"), lax.axis_index("zh")
    scale = 1.0 / T
    c = got[0, :T, :].astype(F32)
    for m in range(1, 16):
        c = c + got[m, :T, :].astype(F32)
    grad_c[...] = c * scale
    a = got[4 * zl, T:, :].astype(F32)
    for j in range(1, 4):
        a = a + got[4 * zl + j, T:, :].astype(F32)
    grad_a[...] = a * scale
    b = b_keep[...]
    for i in range(4):
        b = b + jnp.where(zl == i, 0.0, got[4 * i + zh, T:, :].astype(F32))
    grad_b[...] = b * scale


def cp_kernel(pos, counts, ab, own, oth, obs, res, out_ab, out_own, out_oth,
              acc_ab, acc, obs_v, res_v, in_sem, out_sem):
    slots = obs.shape[0]
    groups = slots // UNROLL
    co = lax.axis_index("co")
    count = counts[0]

    def load(g):
        part = pl.ds(g * UNROLL, UNROLL)
        return pltpu.make_async_copy(obs.at[part], obs_v.at[part], in_sem.at[g])

    def store(g):
        part = pl.ds(g * UNROLL, UNROLL)
        return pltpu.make_async_copy(res_v.at[part], res.at[part], out_sem.at[g])

    for g in range(groups):
        load(g).start()
    acc_ab[...] = jnp.zeros_like(acc_ab)
    acc[...] = jnp.zeros_like(acc)

    def rows(start):
        return pl.ds(pl.multiple_of(start, T), T)

    def places(s):
        pa, pb, pc = pos[0, s], pos[1, s], pos[2, s]
        at_a = (pa & 3) * AB + ((pa >> 2) & 3) * 128 + (pa >> 4) * T
        at_b = (pb & 3) * AB + 512 + (((pb >> 2) & 1) ^ co) * 128 + (pb >> 3) * T
        in_plane = ((pc >> 5) * 4 + ((pc >> 2) & 3)) * T
        return at_a, at_b, pc & 3, in_plane, ((pc >> 4) & 1) ^ co

    def terms(s):
        at_a, at_b, y, in_plane, other = places(s)
        ta = ab[rows(at_a), :]
        tb = ab[rows(at_b), :].astype(F32)
        at_c = rows(y * CY + in_plane)
        tc = jnp.where(other == 0, own[at_c, :].astype(F32), oth[at_c, :].astype(F32))
        pair = (tb[:, None, :] * tc[None, :, :]).reshape(T * T, R).astype(BF)
        model = lax.dot_general(ta, pair, (((1,), (1,)), ((), ())), preferred_element_type=F32)
        live = (s < count).astype(F32)
        resid = (live * (model - obs_v[s].astype(F32))).astype(BF)
        res_v[s] = resid
        term_a = jnp.dot(resid, pair, preferred_element_type=F32)
        wide = lax.dot_general(resid, ta, (((0,), (0,)), ((), ())), preferred_element_type=F32)
        wide = wide.reshape(T, T, R)
        term_b = jnp.sum(wide * tc[None, :, :], axis=1)
        term_c = jnp.sum(wide * tb[:, None, :], axis=0)
        return term_a, term_b, term_c

    def group(g, carry):
        base = g * UNROLL
        load(g).wait()

        @pl.when(base < count)
        def _():
            found = [terms(base + u) for u in range(UNROLL)]
            for u, (term_a, term_b, term_c) in enumerate(found):
                at_a, at_b, y, in_plane, other = places(base + u)
                acc_ab[rows(at_a), :] += term_a
                acc_ab[rows(at_b), :] += term_b
                acc[rows(other * 2048 + y * 512 + in_plane), :] += term_c

        @pl.when(base >= count)
        def _():
            res_v[pl.ds(base, UNROLL)] = jnp.zeros((UNROLL,) + res.shape[1:], BF)

        store(g).start()
        return carry

    lax.fori_loop(0, groups, group, 0)
    out_ab[...] = acc_ab[...].astype(BF)
    out_own[...] = acc[:2048, :]
    out_oth[...] = acc[2048:, :].astype(BF)
    for g in range(groups):
        store(g).wait()


def run_kernel(pos, counts, ab, own, oth, obs):
    slots = obs.shape[0]
    groups = slots // UNROLL
    return pl.pallas_call(
        cp_kernel,
        out_shape=(jax.ShapeDtypeStruct(obs.shape, BF),
                   sds(4 * AB), sds(2048, F32), sds(2048)),
        in_specs=[SMEM, SMEM, VMEM, VMEM, VMEM, HBM],
        out_specs=(HBM, VMEM, VMEM, VMEM),
        scratch_shapes=[
            pltpu.VMEM((4 * AB, R), F32),
            pltpu.VMEM((4096, R), F32),
            pltpu.VMEM(obs.shape, BF),
            pltpu.VMEM(obs.shape, BF),
            pltpu.SemaphoreType.DMA((groups,)),
            pltpu.SemaphoreType.DMA((groups,)),
        ],
        compiler_params=pltpu.CompilerParams(vmem_limit_bytes=48 * 1024 * 1024),
        cost_estimate=pl.CostEstimate(
            flops=slots * 8 * T * T * T * R, bytes_accessed=12_000_000, transcendentals=0
        ),
    )(pos, counts, ab, own, oth, obs)


def on_device(factor_a, factor_b, factor_c, observed, coords, counts):
    slots = observed.shape[3]
    fa, fb, fc = factor_a[0], factor_b[0], factor_c[0]
    swap = [(0, 1), (1, 0)]

    send, b_own = spread(fa, fb, fc)
    got = lax.all_to_all(send, ("zl", "zh"), 0, 0, tiled=True)
    y_send, b_z = small(split_kernel, (sds((4, CY)), sds(128)), got, b_own)
    by_y = lax.all_to_all(y_send, "y", 0, 0, tiled=True)
    b_oth = lax.ppermute(b_z, "co", swap)
    x_send = small(join_kernel, sds(AB), by_y, b_z, b_oth)
    by_y, x_send = lax.optimization_barrier((by_y, x_send))
    by_x = lax.all_gather(x_send, "x", axis=0)
    c_oth = lax.ppermute(by_y, "co", swap)

    res, sum_ab, sum_own, sum_oth = run_kernel(
        coords.reshape(3, slots),
        counts.reshape(1),
        by_x.reshape(4 * AB, R),
        by_y.reshape(4 * CY, R),
        c_oth.reshape(4 * CY, R),
        observed[0, 0, 0],
    )

    ab_in = lax.all_to_all(sum_ab.reshape(4, AB, R), "x", 0, 0, tiled=True)
    c_in = lax.ppermute(sum_oth, "co", swap)
    y_send, b_own, b_send = small(
        pack_y_kernel, (sds((4, CY)), sds(128, F32), sds(128)), ab_in, sum_own, c_in
    )
    ca_in = lax.all_to_all(y_send, "y", 0, 0, tiled=True)
    b_in = lax.ppermute(b_send, "co", swap)
    send, b_keep = small(
        pack_z_kernel, (sds((16, 2 * T)), sds(T, F32)), ca_in, b_own, b_in
    )
    got = lax.all_to_all(send, ("zl", "zh"), 0, 0, tiled=True)
    grad_a, grad_b, grad_c = small(last_kernel, (sds(T, F32),) * 3, got, b_keep)
    return (res.reshape(observed.shape), grad_a[None], grad_b[None], grad_c[None])


def solution(mesh):
    fine = Mesh(mesh.devices.reshape(4, 2, 4, 4, 4), ("zl", "co", "zh", "y", "x"))
    ia, ja = ("zl", "co"), ("zh", "y")
    return jax.shard_map(
        on_device,
        mesh=fine,
        in_specs=(
            P(ia, (*ja, "x"), None),
            P(ja, (*ia, "x"), None),
            P("x", (*ia, *ja), None),
            P(ia, ja, "x", None, None, None),
            P(None, ia, ja, "x", None),
            P(ia, ja, "x"),
        ),
        out_specs=(
            P(ia, ja, "x", None, None, None),
            P(ia, (*ja, "x"), None),
            P(ja, (*ia, "x"), None),
            P("x", (*ia, *ja), None),
        ),
        check_vma=False,
    )
```

time: 147 us -> 137 us (0.932)
  the two profiles are of different devices: /device:TPU:64 before, /device:TPU:32 now
where the time goes in v2:
time: 137 us
  blocking collectives  73.1 us (53%)
  waiting for transfers between devices  23.7 us (17%)
  starting transfers between devices  22.1 us (16%)
  Pallas kernels  15.7 us (11%)
  between operations  1.37 us (1%)
    all_to_all x2, blocking collectives, on_device(): got = lax.all_to_all(send, ('zl', 'zh'), 0, 0, tiled=True)  58.8 us
    all_gather x1, blocking collectives, on_device(): by_x = lax.all_gather(x_send, 'x', axis=0)  14.2 us
    pallas_call x1, Pallas kernels, run_kernel(): pl.pallas_call(cp_kernel, out_shape=(jax.ShapeDtypeStruct(obs.shape, BF),...  11.5 us
    all_to_all x1, waiting for transfers between devices, on_device(): ab_in = lax.all_to_all(sum_ab.reshape(4, AB, R), 'x', 0, 0, tiled=True)  7.72 us
    all_to_all x1, starting transfers between devices, on_device(): ab_in = lax.all_to_all(sum_ab.reshape(4, AB, R), 'x', 0, 0, tiled=True)  6.5 us
    all_to_all x1, waiting for transfers between devices, on_device(): ca_in = lax.all_to_all(y_send, 'y', 0, 0, tiled=True)  6.05 us
    all_to_all x1, waiting for transfers between devices, on_device(): by_y = lax.all_to_all(y_send, 'y', 0, 0, tiled=True)  5.7 us
    all_to_all x1, starting transfers between devices, on_device(): by_y = lax.all_to_all(y_send, 'y', 0, 0, tiled=True)  4.46 us
  transfers between devices with their start and end apart: 7, of which 6 were waited for; matrix products, arithmetic and copies ran while one was open for 0% of the time, Pallas kernels for 0%

profile of v2, /device:TPU:32, one launch (start us, length us, event | category | flops | bytes accessed | tf_op | source)
XLA Modules:
  0.0 136.7 jit_solution(4655346263219737866)
XLA Ops:
  0.6 0.0 copy-start.1
  0.6 1.5 %shard_map.93 = (bf16[16,64,128]{2,1,0:T(8,128)(2,1)}, bf16[32,128]{1,0:T(8,128)(2,1)}) custom-call(bf16[32,128]{1,0:T(8,128)(2,1)} %bitcast.19, bf16[32,128]{1,0:T(8,128)(2,1)} %bitcast.20, bf16[32,128]{1,0:T(8,128)(2,1)} %bitcast.21), custom_call_target="tpu_custom_call" | custom-call | tf_op jit(solution)/shard_map/pallas_call | solution.py:53
  2.2 35.0 %all_to_all.25.got = bf16[16,64,128]{2,1,0:T(8,128)(2,1)S(1)} all-to-all(bf16[16,64,128]{2,1,0:T(8,128)(2,1)} %get-tuple-element.22), channel_id=1, replica_groups=mesh['zl'=4,'co'=2,'zh'=4,'y'=4,'x'=4] {'zl','zh'}, dimensions={0} | all-to-all | bytes 524288 | tf_op jit(solution)/shard_map/all_to_all | solution.py:239
  37.1 0.0 copy-start
  37.1 0.7 copy-done
  37.8 0.9 shard_map.94
  38.7 4.5 %all-to-all-start.1 = ((bf16[4,640,128]{2,1,0:T(8,128)(2,1)}), bf16[4,640,128]{2,1,0:T(8,128)(2,1)S(1)}, u32[]{:S(2)}, u32[]{:S(2)}) async-start(bf16[4,640,128]{2,1,0:T(8,128)(2,1)} %get-tuple-element.24), calls=%async_computation.1 | async-start | bytes 1310720 | tf_op jit(solution)/shard_map/all_to_all | solution.py:241
  43.2 1.9 %collective-permute-start = (bf16[128,128]{1,0:T(8,128)(2,1)S(1)}, bf16[128,128]{1,0:T(8,128)(2,1)S(1)}, u32[]{:S(2)}, u32[]{:S(2)}) collective-permute-start(bf16[128,128]{1,0:T(8,128)(2,1)S(1)} %get-tuple-element.25.b_z), channel_id=1, source_target_pairs={{0,64},{64,0},{1,65},{65,1},{2,66},{66,2},{3,67},{67,3},{4,68},{68... | collective-permute-start | bytes 98312 | tf_op jit(solution)/shard_map/ppermute | solution.py:242
  45.1 1.2 collective-permute-done.b_oth
  46.3 5.7 %all-to-all-done.1.by_y = bf16[4,640,128]{2,1,0:T(8,128)(2,1)S(1)} async-done(((bf16[4,640,128]{2,1,0:T(8,128)(2,1)}), bf16[4,640,128]{2,1,0:T(8,128)(2,1)S(1)}, u32[]{:S(2)}, u32[]{:S(2)}) %all-to-all-start.1) | async-done | bytes 655392 | tf_op jit(solution)/shard_map/all_to_all | solution.py:241
  52.0 1.9 %collective-permute-start.1 = (bf16[4,640,128]{2,1,0:T(8,128)(2,1)S(1)}, bf16[4,640,128]{2,1,0:T(8,128)(2,1)S(1)}, u32[]{:S(2)}, u32[]{:S(2)}) collective-permute-start(bf16[4,640,128]{2,1,0:T(8,128)(2,1)S(1)} %all-to-all-done.1.by_y), channel_id=1, source_target_pairs={{0,64},{64,0},{1,65},{65,1},{2,66},{66,2},{3,67},{67,3},{4,68},{68... | collective-permute-start | bytes 1966088 | tf_op jit(solution)/shard_map/ppermute | solution.py:246
  54.6 0.0 copy-done.1
  54.6 14.2 %all-gather.ab = bf16[3072,128]{1,0:T(8,128)(2,1)S(1)} all-gather(bf16[768,128]{1,0:T(8,128)(2,1)S(1)} %shard_map.95), channel_id=2, replica_groups=mesh['zl'=4,'co'=2,'zh'=4,'y'=4,'x'=4] {'x'}, dimensions={0}, use_global_device_ids=true | all-gather | bytes 983040 | tf_op jit(solution)/shard_map/all_gather | solution.py:245
  68.8 0.0 collective-permute-done.1
  68.8 11.5 %shard_map.96 = (bf16[36,32,1024]{2,1,0:T(8,128)(2,1)}, bf16[3072,128]{1,0:T(8,128)(2,1)}, f32[2048,128]{1,0:T(8,128)S(1)}, bf16[2048,128]{1,0:T(8,128)(2,1)S(1)}) custom-call(s32[3,36]{1,0:T(4,128)S(1)} %bitcast.17, s32[1]{0:T(128)} %bitcast.15.counts, bf16[3072,128]{1,0:T(8,128)(2,1)S(1)} %all-gather.ab, bf16[2560,128]{1,0:T(8,128)(2,1)S(1)} %bitcast.16, ...), custom_call_target="tpu_custom_call" | custom-call | flops 1207959552 | bytes 12000000 | tf_op jit(solution)/shard_map/pallas_call | solution.py:212
  80.4 6.5 %all-to-all-start.2 = ((bf16[4,768,128]{2,1,0:T(8,128)(2,1)}), bf16[4,768,128]{2,1,0:T(8,128)(2,1)S(1)}, u32[]{:S(2)}, u32[]{:S(2)}) async-start(bf16[4,768,128]{2,1,0:T(8,128)(2,1)} %bitcast.8), calls=%async_computation.2 | async-start | bytes 1572864 | tf_op jit(solution)/shard_map/all_to_all | solution.py:257
  86.9 1.9 %collective-permute-start.2 = (bf16[2048,128]{1,0:T(8,128)(2,1)S(1)}, bf16[2048,128]{1,0:T(8,128)(2,1)S(1)}, u32[]{:S(2)}, u32[]{:S(2)}) collective-permute-start(bf16[2048,128]{1,0:T(8,128)(2,1)S(1)} %get-tuple-element.31), channel_id=1, source_target_pairs={{0,64},{64,0},{1,65},{65,1},{2,66},{66,2},{3,67},{67,3},{4,68},{68... | collective-permute-start | bytes 1572872 | tf_op jit(solution)/shard_map/ppermute | solution.py:258
  88.8 1.9 %collective-permute-done.2.c_in = bf16[2048,128]{1,0:T(8,128)(2,1)S(1)} collective-permute-done((bf16[2048,128]{1,0:T(8,128)(2,1)S(1)}, bf16[2048,128]{1,0:T(8,128)(2,1)S(1)}, u32[]{:S(2)}, u32[]{:S(2)}) %collective-permute-start.2) | collective-permute-done | bytes 524320 | tf_op jit(solution)/shard_map/ppermute | solution.py:258
  90.7 7.7 %all-to-all-done.2.ab_in = bf16[4,768,128]{2,1,0:T(8,128)(2,1)S(1)} async-done(((bf16[4,768,128]{2,1,0:T(8,128)(2,1)}), bf16[4,768,128]{2,1,0:T(8,128)(2,1)S(1)}, u32[]{:S(2)}, u32[]{:S(2)}) %all-to-all-start.2) | async-done | bytes 786464 | tf_op jit(solution)/shard_map/all_to_all | solution.py:257
  98.4 1.0 shard_map.97
  99.4 3.5 %all-to-all-start.3 = ((bf16[4,640,128]{2,1,0:T(8,128)(2,1)}), bf16[4,640,128]{2,1,0:T(8,128)(2,1)S(1)}, u32[]{:S(2)}, u32[]{:S(2)}) async-start(bf16[4,640,128]{2,1,0:T(8,128)(2,1)} %get-tuple-element.32), calls=%async_computation.3 | async-start | bytes 1310720 | tf_op jit(solution)/shard_map/all_to_all | solution.py:262
  102.9 1.9 %collective-permute-start.3 = (bf16[128,128]{1,0:T(8,128)(2,1)S(1)}, bf16[128,128]{1,0:T(8,128)(2,1)S(1)}, u32[]{:S(2)}, u32[]{:S(2)}) collective-permute-start(bf16[128,128]{1,0:T(8,128)(2,1)S(1)} %get-tuple-element.34), channel_id=1, source_target_pairs={{0,64},{64,0},{1,65},{65,1},{2,66},{66,2},{3,67},{67,3},{4,68},{68... | collective-permute-start | bytes 98312 | tf_op jit(solution)/shard_map/ppermute | solution.py:263
  104.8 1.2 collective-permute-done.3.b_in
  106.0 6.1 %all-to-all-done.3.ca_in = bf16[4,640,128]{2,1,0:T(8,128)(2,1)S(1)} async-done(((bf16[4,640,128]{2,1,0:T(8,128)(2,1)}), bf16[4,640,128]{2,1,0:T(8,128)(2,1)S(1)}, u32[]{:S(2)}, u32[]{:S(2)}) %all-to-all-start.3) | async-done | bytes 655392 | tf_op jit(solution)/shard_map/all_to_all | solution.py:262
  112.1 0.1 shard_map.98
  112.2 23.9 %all_to_all.26.got = bf16[16,64,128]{2,1,0:T(8,128)(2,1)S(1)} all-to-all(bf16[16,64,128]{2,1,0:T(8,128)(2,1)S(1)} %get-tuple-element.35), channel_id=1, replica_groups=mesh['zl'=4,'co'=2,'zh'=4,'y'=4,'x'=4] {'zl','zh'}, dimensions={0} | all-to-all | bytes 524288 | tf_op jit(solution)/shard_map/all_to_all | solution.py:267
  136.0 0.6 shard_map.99
  (2 shorter events, 0.0 us)
Async XLA Ops:
  0.6 54.0 %copy-start.1 = (s32[3,1,1,1,36]{4,3,2,1,0:T(1,128)S(1)}, s32[3,1,1,1,36]{4,3,2,1,0:T(1,128)}, u32[]{:S(2)}) copy-start(s32[3,1,1,1,36]{4,3,2,1,0:T(1,128)} %param.10) | copy-start | bytes 1300
  37.1 0.7 copy-start
  38.7 13.2 %all-to-all-start.1 = ((bf16[4,640,128]{2,1,0:T(8,128)(2,1)}), bf16[4,640,128]{2,1,0:T(8,128)(2,1)S(1)}, u32[]{:S(2)}, u32[]{:S(2)}) async-start(bf16[4,640,128]{2,1,0:T(8,128)(2,1)} %get-tuple-element.24), calls=%async_computation.1 | async-start | bytes 1310720 | tf_op jit(solution)/shard_map/all_to_all | solution.py:241
  43.2 3.1 %collective-permute-start = (bf16[128,128]{1,0:T(8,128)(2,1)S(1)}, bf16[128,128]{1,0:T(8,128)(2,1)S(1)}, u32[]{:S(2)}, u32[]{:S(2)}) collective-permute-start(bf16[128,128]{1,0:T(8,128)(2,1)S(1)} %get-tuple-element.25.b_z), channel_id=1, source_target_pairs={{0,64},{64,0},{1,65},{65,1},{2,66},{66,2},{3,67},{67,3},{4,68},{68... | collective-permute-start | bytes 98312 | tf_op jit(solution)/shard_map/ppermute | solution.py:242
  52.0 16.8 %collective-permute-start.1 = (bf16[4,640,128]{2,1,0:T(8,128)(2,1)S(1)}, bf16[4,640,128]{2,1,0:T(8,128)(2,1)S(1)}, u32[]{:S(2)}, u32[]{:S(2)}) collective-permute-start(bf16[4,640,128]{2,1,0:T(8,128)(2,1)S(1)} %all-to-all-done.1.by_y), channel_id=1, source_target_pairs={{0,64},{64,0},{1,65},{65,1},{2,66},{66,2},{3,67},{67,3},{4,68},{68... | collective-permute-start | bytes 1966088 | tf_op jit(solution)/shard_map/ppermute | solution.py:246
  80.4 18.0 %all-to-all-start.2 = ((bf16[4,768,128]{2,1,0:T(8,128)(2,1)}), bf16[4,768,128]{2,1,0:T(8,128)(2,1)S(1)}, u32[]{:S(2)}, u32[]{:S(2)}) async-start(bf16[4,768,128]{2,1,0:T(8,128)(2,1)} %bitcast.8), calls=%async_computation.2 | async-start | bytes 1572864 | tf_op jit(solution)/shard_map/all_to_all | solution.py:257
  86.9 3.8 %collective-permute-start.2 = (bf16[2048,128]{1,0:T(8,128)(2,1)S(1)}, bf16[2048,128]{1,0:T(8,128)(2,1)S(1)}, u32[]{:S(2)}, u32[]{:S(2)}) collective-permute-start(bf16[2048,128]{1,0:T(8,128)(2,1)S(1)} %get-tuple-element.31), channel_id=1, source_target_pairs={{0,64},{64,0},{1,65},{65,1},{2,66},{66,2},{3,67},{67,3},{4,68},{68... | collective-permute-start | bytes 1572872 | tf_op jit(solution)/shard_map/ppermute | solution.py:258
  99.4 12.6 %all-to-all-start.3 = ((bf16[4,640,128]{2,1,0:T(8,128)(2,1)}), bf16[4,640,128]{2,1,0:T(8,128)(2,1)S(1)}, u32[]{:S(2)}, u32[]{:S(2)}) async-start(bf16[4,640,128]{2,1,0:T(8,128)(2,1)} %get-tuple-element.32), calls=%async_computation.3 | async-start | bytes 1310720 | tf_op jit(solution)/shard_map/all_to_all | solution.py:262
  102.9 3.1 %collective-permute-start.3 = (bf16[128,128]{1,0:T(8,128)(2,1)S(1)}, bf16[128,128]{1,0:T(8,128)(2,1)S(1)}, u32[]{:S(2)}, u32[]{:S(2)}) collective-permute-start(bf16[128,128]{1,0:T(8,128)(2,1)S(1)} %get-tuple-element.34), channel_id=1, source_target_pairs={{0,64},{64,0},{1,65},{65,1},{2,66},{66,2},{3,67},{67,3},{4,68},{68... | collective-permute-start | bytes 98312 | tf_op jit(solution)/shard_map/ppermute | solution.py:263

commit v3 on v2

--- a/solution.py
+++ b/solution.py
@@ -9,7 +9,7 @@
 F32 = jnp.float32
 T = 32
 R = 128
-UNROLL = 4
+UNROLL = 12
 VMEM = pl.BlockSpec(memory_space=pltpu.VMEM)
 SMEM = pl.BlockSpec(memory_space=pltpu.SMEM)
 HBM = pl.BlockSpec(memory_space=pltpu.HBM)
@@ -32,48 +32,60 @@
     )(*args)
 
 
-def spread_kernel(fa, fb, fc, send, b_own, a_v, c_v, sem):
+def spread_kernel(fa, fb, fc, send, a_v, b_v, c_v, sem):
     zl = lax.axis_index("zl")
     copies = [
         pltpu.make_async_copy(src, dst, sem.at[n])
-        for n, (src, dst) in enumerate(((fa, a_v), (fb, b_own), (fc, c_v)))
+        for n, (src, dst) in enumerate(((fa, a_v), (fb, b_v), (fc, c_v)))
     ]
     for copy in copies:
         copy.start()
     for copy in copies:
         copy.wait()
     for i in range(4):
-        second = jnp.where(zl == i, a_v[...], b_own[...])
+        second = jnp.where(zl == i, a_v[...], b_v[...])
         for j in range(4):
-            send[4 * i + j, :T, :] = c_v[...]
-            send[4 * i + j, T:, :] = second
+            send[4 * j + i, :T, :] = c_v[...]
+            send[4 * j + i, T:, :] = second
 
 
 def spread(fa, fb, fc):
     return pl.pallas_call(
         spread_kernel,
-        out_shape=(sds((16, 2 * T)), sds(T)),
+        out_shape=sds((16, 2 * T)),
         in_specs=[HBM, HBM, HBM],
-        out_specs=(VMEM, VMEM),
-        scratch_shapes=[
-            pltpu.VMEM((T, R), BF), pltpu.VMEM((T, R), BF), pltpu.SemaphoreType.DMA((3,))
-        ],
+        out_specs=VMEM,
+        scratch_shapes=[pltpu.VMEM((T, R), BF)] * 3 + [pltpu.SemaphoreType.DMA((3,))],
         compiler_params=pltpu.CompilerParams(vmem_limit_bytes=60 * 1024 * 1024),
     )(fa, fb, fc)
 
 
-def split_kernel(got, b_own, y_send, b_z):
+def split_kernel(got, fb, y_send, b_z, b_v, sem):
+    own = pltpu.make_async_copy(fb, b_v, sem)
+    own.start()
     zl, zh = lax.axis_index("zl"), lax.axis_index("zh")
     for m in range(16):
         tile = got[m, :T, :]
         for k in range(4):
             y_send[k, m * T : (m + 1) * T, :] = tile
     for j in range(4):
-        tile = got[4 * zl + j, T:, :]
+        tile = got[4 * j + zl, T:, :]
         for k in range(4):
             y_send[k, 512 + j * T : 512 + (j + 1) * T, :] = tile
+    own.wait()
     for i in range(4):
-        b_z[i * T : (i + 1) * T, :] = jnp.where(zl == i, b_own[...], got[4 * i + zh, T:, :])
+        b_z[i * T : (i + 1) * T, :] = jnp.where(zl == i, b_v[...], got[4 * zh + i, T:, :])
+
+
+def split(got, fb):
+    return pl.pallas_call(
+        split_kernel,
+        out_shape=(sds((4, CY)), sds(128)),
+        in_specs=[VMEM, HBM],
+        out_specs=(VMEM, VMEM),
+        scratch_shapes=[pltpu.VMEM((T, R), BF), pltpu.SemaphoreType.DMA],
+        compiler_params=pltpu.CompilerParams(vmem_limit_bytes=48 * 1024 * 1024),
+    )(got, fb)
 
 
 def join_kernel(by_y, b_z, b_oth, x_send):
@@ -106,7 +118,7 @@
         rows = slice(i * T, (i + 1) * T)
         b = b_own[rows, :] + b_in[rows, :].astype(F32)
         for j in range(4):
-            send[4 * i + j, T:, :] = jnp.where(zl == i, a[j], b).astype(BF)
+            send[4 * j + i, T:, :] = jnp.where(zl == i, a[j], b).astype(BF)
 
         @pl.when(zl == i)
         def _():
@@ -120,13 +132,13 @@
     for m in range(1, 16):
         c = c + got[m, :T, :].astype(F32)
     grad_c[...] = c * scale
-    a = got[4 * zl, T:, :].astype(F32)
+    a = got[zl, T:, :].astype(F32)
     for j in range(1, 4):
-        a = a + got[4 * zl + j, T:, :].astype(F32)
+        a = a + got[4 * j + zl, T:, :].astype(F32)
     grad_a[...] = a * scale
     b = b_keep[...]
     for i in range(4):
-        b = b + jnp.where(zl == i, 0.0, got[4 * i + zh, T:, :].astype(F32))
+        b = b + jnp.where(zl == i, 0.0, got[4 * zh + i, T:, :].astype(F32))
     grad_b[...] = b * scale
 
 
@@ -157,26 +169,42 @@
         pa, pb, pc = pos[0, s], pos[1, s], pos[2, s]
         at_a = (pa & 3) * AB + ((pa >> 2) & 3) * 128 + (pa >> 4) * T
         at_b = (pb & 3) * AB + 512 + (((pb >> 2) & 1) ^ co) * 128 + (pb >> 3) * T
-        in_plane = ((pc >> 5) * 4 + ((pc >> 2) & 3)) * T
+        in_plane = (((pc >> 2) & 3) * 4 + (pc >> 5)) * T
         return at_a, at_b, pc & 3, in_plane, ((pc >> 4) & 1) ^ co
 
-    def terms(s):
+    def tiles(s):
         at_a, at_b, y, in_plane, other = places(s)
-        ta = ab[rows(at_a), :]
-        tb = ab[rows(at_b), :].astype(F32)
         at_c = rows(y * CY + in_plane)
         tc = jnp.where(other == 0, own[at_c, :].astype(F32), oth[at_c, :].astype(F32))
-        pair = (tb[:, None, :] * tc[None, :, :]).reshape(T * T, R).astype(BF)
+        return ab[rows(at_a), :], ab[rows(at_b), :].astype(F32), tc
+
+    def two(s):
+        (ta0, tb0, tc0), (ta1, tb1, tc1) = tiles(s), tiles(s + 1)
+        none = jnp.zeros((T, R), BF)
+        ta = jnp.concatenate(
+            [jnp.concatenate([ta0, none], axis=1), jnp.concatenate([none, ta1], axis=1)], axis=0
+        )
+        tb = jnp.concatenate([tb0, tb1], axis=1)
+        tc = jnp.concatenate([tc0, tc1], axis=1)
+        pair = (tb[:, None, :] * tc[None, :, :]).reshape(T * T, 2 * R).astype(BF)
         model = lax.dot_general(ta, pair, (((1,), (1,)), ((), ())), preferred_element_type=F32)
-        live = (s < count).astype(F32)
-        resid = (live * (model - obs_v[s].astype(F32))).astype(BF)
-        res_v[s] = resid
+        resids = []
+        for u in range(2):
+            live = (s + u < count).astype(F32)
+            part = live * (model[u * T : (u + 1) * T, :] - obs_v[s + u].astype(F32))
+            resids.append(part.astype(BF))
+            res_v[s + u] = resids[u]
+        resid = jnp.concatenate(resids, axis=0)
         term_a = jnp.dot(resid, pair, preferred_element_type=F32)
         wide = lax.dot_general(resid, ta, (((0,), (0,)), ((), ())), preferred_element_type=F32)
-        wide = wide.reshape(T, T, R)
+        wide = wide.reshape(T, T, 2 * R)
         term_b = jnp.sum(wide * tc[None, :, :], axis=1)
         term_c = jnp.sum(wide * tb[:, None, :], axis=0)
-        return term_a, term_b, term_c
+        return [
+            (term_a[u * T : (u + 1) * T, u * R : (u + 1) * R],
+             term_b[:, u * R : (u + 1) * R], term_c[:, u * R : (u + 1) * R])
+            for u in range(2)
+        ]
 
     def group(g, carry):
         base = g * UNROLL
@@ -184,7 +212,7 @@
 
         @pl.when(base < count)
         def _():
-            found = [terms(base + u) for u in range(UNROLL)]
+            found = [t for u in range(0, UNROLL, 2) for t in two(base + u)]
             for u, (term_a, term_b, term_c) in enumerate(found):
                 at_a, at_b, y, in_plane, other = places(base + u)
                 acc_ab[rows(at_a), :] += term_a
@@ -235,9 +263,9 @@
     fa, fb, fc = factor_a[0], factor_b[0], factor_c[0]
     swap = [(0, 1), (1, 0)]
 
-    send, b_own = spread(fa, fb, fc)
-    got = lax.all_to_all(send, ("zl", "zh"), 0, 0, tiled=True)
-    y_send, b_z = small(split_kernel, (sds((4, CY)), sds(128)), got, b_own)
+    send = spread(fa, fb, fc)
+    got = lax.all_to_all(send, ("zh", "zl"), 0, 0, tiled=True)
+    y_send, b_z = split(got, fb)
     by_y = lax.all_to_all(y_send, "y", 0, 0, tiled=True)
     b_oth = lax.ppermute(b_z, "co", swap)
     x_send = small(join_kernel, sds(AB), by_y, b_z, b_oth)
@@ -264,7 +292,7 @@
     send, b_keep = small(
         pack_z_kernel, (sds((16, 2 * T)), sds(T, F32)), ca_in, b_own, b_in
     )
-    got = lax.all_to_all(send, ("zl", "zh"), 0, 0, tiled=True)
+    got = lax.all_to_all(send, ("zh", "zl"), 0, 0, tiled=True)
     grad_a, grad_b, grad_c = small(last_kernel, (sds(T, F32),) * 3, got, b_keep)
     return (res.reshape(observed.shape), grad_a[None], grad_b[None], grad_c[None])
 

time: 137 us -> 132 us (0.964)
  blocking collectives: 73.1 us -> 70 us
  starting transfers between devices: 22.1 us -> 19.1 us
    all_to_all x2, blocking collectives: 58.8 us -> 55.8 us  [on_device(): got = lax.all_to_all(send, ('zh', 'zl'), 0, 0, tiled=True)]
    all_to_all x1, starting transfers between devices: 6.5 us -> 3.5 us  [on_device(): ab_in = lax.all_to_all(sum_ab.reshape(4, AB, R), 'x', 0, 0, tiled=True)]
where the time goes in v3:
time: 132 us; the launch traced here: 131 us
  blocking collectives  70 us (53%)
  waiting for transfers between devices  23.8 us (18%)
  starting transfers between devices  19.1 us (14%)
  Pallas kernels  16.3 us (12%)
  between operations  1.39 us (1%)
    all_to_all x2, blocking collectives, on_device(): got = lax.all_to_all(send, ('zh', 'zl'), 0, 0, tiled=True)  55.8 us
    all_gather x1, blocking collectives, on_device(): by_x = lax.all_gather(x_send, 'x', axis=0)  14.2 us
    pallas_call x1, Pallas kernels, run_kernel(): pl.pallas_call(cp_kernel, out_shape=(jax.ShapeDtypeStruct(obs.shape, BF),...  12.1 us
    all_to_all x1, waiting for transfers between devices, on_device(): by_y = lax.all_to_all(y_send, 'y', 0, 0, tiled=True)  6.96 us
    all_to_all x1, waiting for transfers between devices, on_device(): ab_in = lax.all_to_all(sum_ab.reshape(4, AB, R), 'x', 0, 0, tiled=True)  6.93 us
    all_to_all x1, waiting for transfers between devices, on_device(): ca_in = lax.all_to_all(y_send, 'y', 0, 0, tiled=True)  5.65 us
    all_to_all x1, starting transfers between devices, on_device(): by_y = lax.all_to_all(y_send, 'y', 0, 0, tiled=True)  4.48 us
    all_to_all x1, starting transfers between devices, on_device(): ab_in = lax.all_to_all(sum_ab.reshape(4, AB, R), 'x', 0, 0, tiled=True)  3.5 us
  transfers between devices with their start and end apart: 7, of which 6 were waited for; matrix products, arithmetic and copies ran while one was open for 0% of the time, Pallas kernels for 0%

profile of v3, /device:TPU:32, one launch (start us, length us, event | category | flops | bytes accessed | tf_op | source)
XLA Modules:
  0.0 131.4 jit_solution(10197062734143598880)
XLA Ops:
  0.6 0.0 copy-start.1
  0.6 1.5 %shard_map.93 = bf16[16,64,128]{2,1,0:T(8,128)(2,1)} custom-call(bf16[32,128]{1,0:T(8,128)(2,1)} %bitcast.21, bf16[32,128]{1,0:T(8,128)(2,1)} %bitcast.17, bf16[32,128]{1,0:T(8,128)(2,1)} %bitcast.22), custom_call_target="tpu_custom_call" | custom-call | tf_op jit(solution)/shard_map/pallas_call | solution.py:53
  2.1 33.1 %all_to_all.25.got = bf16[16,64,128]{2,1,0:T(8,128)(2,1)S(1)} all-to-all(bf16[16,64,128]{2,1,0:T(8,128)(2,1)} %shard_map.93), channel_id=1, replica_groups=mesh['zl'=4,'co'=2,'zh'=4,'y'=4,'x'=4] {'zh','zl'}, dimensions={0} | all-to-all | bytes 524288 | tf_op jit(solution)/shard_map/all_to_all | solution.py:267
  35.3 0.0 copy-start
  35.3 0.7 copy-done
  36.0 0.9 shard_map.94
  36.9 4.5 %all-to-all-start.1 = ((bf16[4,640,128]{2,1,0:T(8,128)(2,1)}), bf16[4,640,128]{2,1,0:T(8,128)(2,1)S(1)}, u32[]{:S(2)}, u32[]{:S(2)}) async-start(bf16[4,640,128]{2,1,0:T(8,128)(2,1)} %get-tuple-element.20), calls=%async_computation.1 | async-start | bytes 1310720 | tf_op jit(solution)/shard_map/all_to_all | solution.py:269
  41.4 1.9 %collective-permute-start = (bf16[128,128]{1,0:T(8,128)(2,1)S(1)}, bf16[128,128]{1,0:T(8,128)(2,1)S(1)}, u32[]{:S(2)}, u32[]{:S(2)}) collective-permute-start(bf16[128,128]{1,0:T(8,128)(2,1)S(1)} %get-tuple-element.21.b_z), channel_id=1, source_target_pairs={{0,64},{64,0},{1,65},{65,1},{2,66},{66,2},{3,67},{67,3},{4,68},{68... | collective-permute-start | bytes 98312 | tf_op jit(solution)/shard_map/ppermute | solution.py:270
  43.3 1.2 collective-permute-done.b_oth
  44.5 7.0 %all-to-all-done.1.by_y = bf16[4,640,128]{2,1,0:T(8,128)(2,1)S(1)} async-done(((bf16[4,640,128]{2,1,0:T(8,128)(2,1)}), bf16[4,640,128]{2,1,0:T(8,128)(2,1)S(1)}, u32[]{:S(2)}, u32[]{:S(2)}) %all-to-all-start.1) | async-done | bytes 655392 | tf_op jit(solution)/shard_map/all_to_all | solution.py:269
  51.5 1.9 %collective-permute-start.1 = (bf16[4,640,128]{2,1,0:T(8,128)(2,1)S(1)}, bf16[4,640,128]{2,1,0:T(8,128)(2,1)S(1)}, u32[]{:S(2)}, u32[]{:S(2)}) collective-permute-start(bf16[4,640,128]{2,1,0:T(8,128)(2,1)S(1)} %all-to-all-done.1.by_y), channel_id=1, source_target_pairs={{0,64},{64,0},{1,65},{65,1},{2,66},{66,2},{3,67},{67,3},{4,68},{68... | collective-permute-start | bytes 1966088 | tf_op jit(solution)/shard_map/ppermute | solution.py:274
  54.0 0.0 copy-done.1
  54.1 14.2 %all-gather.ab = bf16[3072,128]{1,0:T(8,128)(2,1)S(1)} all-gather(bf16[768,128]{1,0:T(8,128)(2,1)S(1)} %shard_map.95), channel_id=2, replica_groups=mesh['zl'=4,'co'=2,'zh'=4,'y'=4,'x'=4] {'x'}, dimensions={0}, use_global_device_ids=true | all-gather | bytes 983040 | tf_op jit(solution)/shard_map/all_gather | solution.py:273
  68.3 0.0 collective-permute-done.1
  68.3 12.1 %shard_map.96 = (bf16[36,32,1024]{2,1,0:T(8,128)(2,1)}, bf16[3072,128]{1,0:T(8,128)(2,1)}, f32[2048,128]{1,0:T(8,128)S(1)}, bf16[2048,128]{1,0:T(8,128)(2,1)S(1)}) custom-call(s32[3,36]{1,0:T(4,128)S(1)} %bitcast.19, s32[1]{0:T(128)} %bitcast.15.counts, bf16[3072,128]{1,0:T(8,128)(2,1)S(1)} %all-gather.ab, bf16[2560,128]{1,0:T(8,128)(2,1)S(1)} %bitcast.16, ...), custom_call_target="tpu_custom_call" | custom-call | flops 1207959552 | bytes 12000000 | tf_op jit(solution)/shard_map/pallas_call | solution.py:240
  80.4 3.5 %all-to-all-start.2 = ((bf16[4,768,128]{2,1,0:T(8,128)(2,1)}), bf16[4,768,128]{2,1,0:T(8,128)(2,1)S(1)}, u32[]{:S(2)}, u32[]{:S(2)}) async-start(bf16[4,768,128]{2,1,0:T(8,128)(2,1)} %bitcast.8), calls=%async_computation.2 | async-start | bytes 1572864 | tf_op jit(solution)/shard_map/all_to_all | solution.py:285
  83.9 1.9 %collective-permute-start.2 = (bf16[2048,128]{1,0:T(8,128)(2,1)S(1)}, bf16[2048,128]{1,0:T(8,128)(2,1)S(1)}, u32[]{:S(2)}, u32[]{:S(2)}) collective-permute-start(bf16[2048,128]{1,0:T(8,128)(2,1)S(1)} %get-tuple-element.27), channel_id=1, source_target_pairs={{0,64},{64,0},{1,65},{65,1},{2,66},{66,2},{3,67},{67,3},{4,68},{68... | collective-permute-start | bytes 1572872 | tf_op jit(solution)/shard_map/ppermute | solution.py:286
  85.9 1.9 %collective-permute-done.2.c_in = bf16[2048,128]{1,0:T(8,128)(2,1)S(1)} collective-permute-done((bf16[2048,128]{1,0:T(8,128)(2,1)S(1)}, bf16[2048,128]{1,0:T(8,128)(2,1)S(1)}, u32[]{:S(2)}, u32[]{:S(2)}) %collective-permute-start.2) | collective-permute-done | bytes 524320 | tf_op jit(solution)/shard_map/ppermute | solution.py:286
  87.7 6.9 %all-to-all-done.2.ab_in = bf16[4,768,128]{2,1,0:T(8,128)(2,1)S(1)} async-done(((bf16[4,768,128]{2,1,0:T(8,128)(2,1)}), bf16[4,768,128]{2,1,0:T(8,128)(2,1)S(1)}, u32[]{:S(2)}, u32[]{:S(2)}) %all-to-all-start.2) | async-done | bytes 786464 | tf_op jit(solution)/shard_map/all_to_all | solution.py:285
  94.7 1.0 shard_map.97
  95.7 3.5 %all-to-all-start.3 = ((bf16[4,640,128]{2,1,0:T(8,128)(2,1)}), bf16[4,640,128]{2,1,0:T(8,128)(2,1)S(1)}, u32[]{:S(2)}, u32[]{:S(2)}) async-start(bf16[4,640,128]{2,1,0:T(8,128)(2,1)} %get-tuple-element.28), calls=%async_computation.3 | async-start | bytes 1310720 | tf_op jit(solution)/shard_map/all_to_all | solution.py:290
  99.2 1.9 %collective-permute-start.3 = (bf16[128,128]{1,0:T(8,128)(2,1)S(1)}, bf16[128,128]{1,0:T(8,128)(2,1)S(1)}, u32[]{:S(2)}, u32[]{:S(2)}) collective-permute-start(bf16[128,128]{1,0:T(8,128)(2,1)S(1)} %get-tuple-element.30), channel_id=1, source_target_pairs={{0,64},{64,0},{1,65},{65,1},{2,66},{66,2},{3,67},{67,3},{4,68},{68... | collective-permute-start | bytes 98312 | tf_op jit(solution)/shard_map/ppermute | solution.py:291
  101.1 1.2 collective-permute-done.3.b_in
  102.3 5.6 %all-to-all-done.3.ca_in = bf16[4,640,128]{2,1,0:T(8,128)(2,1)S(1)} async-done(((bf16[4,640,128]{2,1,0:T(8,128)(2,1)}), bf16[4,640,128]{2,1,0:T(8,128)(2,1)S(1)}, u32[]{:S(2)}, u32[]{:S(2)}) %all-to-all-start.3) | async-done | bytes 655392 | tf_op jit(solution)/shard_map/all_to_all | solution.py:290
  107.9 0.1 shard_map.98
  108.0 22.7 %all_to_all.26.got = bf16[16,64,128]{2,1,0:T(8,128)(2,1)S(1)} all-to-all(bf16[16,64,128]{2,1,0:T(8,128)(2,1)S(1)} %get-tuple-element.31), channel_id=1, replica_groups=mesh['zl'=4,'co'=2,'zh'=4,'y'=4,'x'=4] {'zh','zl'}, dimensions={0} | all-to-all | bytes 524288 | tf_op jit(solution)/shard_map/all_to_all | solution.py:295
  130.7 0.6 shard_map.99
  (2 shorter events, 0.0 us)
Async XLA Ops:
  0.6 53.4 %copy-start.1 = (s32[3,1,1,1,36]{4,3,2,1,0:T(1,128)S(1)}, s32[3,1,1,1,36]{4,3,2,1,0:T(1,128)}, u32[]{:S(2)}) copy-start(s32[3,1,1,1,36]{4,3,2,1,0:T(1,128)} %param.10) | copy-start | bytes 1300
  35.3 0.7 copy-start
  36.9 14.5 %all-to-all-start.1 = ((bf16[4,640,128]{2,1,0:T(8,128)(2,1)}), bf16[4,640,128]{2,1,0:T(8,128)(2,1)S(1)}, u32[]{:S(2)}, u32[]{:S(2)}) async-start(bf16[4,640,128]{2,1,0:T(8,128)(2,1)} %get-tuple-element.20), calls=%async_computation.1 | async-start | bytes 1310720 | tf_op jit(solution)/shard_map/all_to_all | solution.py:269
  41.4 3.1 %collective-permute-start = (bf16[128,128]{1,0:T(8,128)(2,1)S(1)}, bf16[128,128]{1,0:T(8,128)(2,1)S(1)}, u32[]{:S(2)}, u32[]{:S(2)}) collective-permute-start(bf16[128,128]{1,0:T(8,128)(2,1)S(1)} %get-tuple-element.21.b_z), channel_id=1, source_target_pairs={{0,64},{64,0},{1,65},{65,1},{2,66},{66,2},{3,67},{67,3},{4,68},{68... | collective-permute-start | bytes 98312 | tf_op jit(solution)/shard_map/ppermute | solution.py:270
  51.5 16.8 %collective-permute-start.1 = (bf16[4,640,128]{2,1,0:T(8,128)(2,1)S(1)}, bf16[4,640,128]{2,1,0:T(8,128)(2,1)S(1)}, u32[]{:S(2)}, u32[]{:S(2)}) collective-permute-start(bf16[4,640,128]{2,1,0:T(8,128)(2,1)S(1)} %all-to-all-done.1.by_y), channel_id=1, source_target_pairs={{0,64},{64,0},{1,65},{65,1},{2,66},{66,2},{3,67},{67,3},{4,68},{68... | collective-permute-start | bytes 1966088 | tf_op jit(solution)/shard_map/ppermute | solution.py:274
  80.4 14.2 %all-to-all-start.2 = ((bf16[4,768,128]{2,1,0:T(8,128)(2,1)}), bf16[4,768,128]{2,1,0:T(8,128)(2,1)S(1)}, u32[]{:S(2)}, u32[]{:S(2)}) async-start(bf16[4,768,128]{2,1,0:T(8,128)(2,1)} %bitcast.8), calls=%async_computation.2 | async-start | bytes 1572864 | tf_op jit(solution)/shard_map/all_to_all | solution.py:285
  83.9 3.8 %collective-permute-start.2 = (bf16[2048,128]{1,0:T(8,128)(2,1)S(1)}, bf16[2048,128]{1,0:T(8,128)(2,1)S(1)}, u32[]{:S(2)}, u32[]{:S(2)}) collective-permute-start(bf16[2048,128]{1,0:T(8,128)(2,1)S(1)} %get-tuple-element.27), channel_id=1, source_target_pairs={{0,64},{64,0},{1,65},{65,1},{2,66},{66,2},{3,67},{67,3},{4,68},{68... | collective-permute-start | bytes 1572872 | tf_op jit(solution)/shard_map/ppermute | solution.py:286
  95.7 12.2 %all-to-all-start.3 = ((bf16[4,640,128]{2,1,0:T(8,128)(2,1)}), bf16[4,640,128]{2,1,0:T(8,128)(2,1)S(1)}, u32[]{:S(2)}, u32[]{:S(2)}) async-start(bf16[4,640,128]{2,1,0:T(8,128)(2,1)} %get-tuple-element.28), calls=%async_computation.3 | async-start | bytes 1310720 | tf_op jit(solution)/shard_map/all_to_all | solution.py:290
  99.2 3.1 %collective-permute-start.3 = (bf16[128,128]{1,0:T(8,128)(2,1)S(1)}, bf16[128,128]{1,0:T(8,128)(2,1)S(1)}, u32[]{:S(2)}, u32[]{:S(2)}) collective-permute-start(bf16[128,128]{1,0:T(8,128)(2,1)S(1)} %get-tuple-element.30), channel_id=1, source_target_pairs={{0,64},{64,0},{1,65},{65,1},{2,66},{66,2},{3,67},{67,3},{4,68},{68... | collective-permute-start | bytes 98312 | tf_op jit(solution)/shard_map/ppermute | solution.py:291

commit v4 on v3

--- a/solution.py
+++ b/solution.py
@@ -9,7 +9,7 @@
 F32 = jnp.float32
 T = 32
 R = 128
-UNROLL = 12
+UNROLL = 36
 VMEM = pl.BlockSpec(memory_space=pltpu.VMEM)
 SMEM = pl.BlockSpec(memory_space=pltpu.SMEM)
 HBM = pl.BlockSpec(memory_space=pltpu.HBM)
@@ -60,9 +60,25 @@
     )(fa, fb, fc)
 
 
-def split_kernel(got, fb, y_send, b_z, b_v, sem):
-    own = pltpu.make_async_copy(fb, b_v, sem)
-    own.start()
+def fetch_kernel(fb, b_own, sem):
+    copy = pltpu.make_async_copy(fb, b_own, sem)
+    copy.start()
+    copy.wait()
+
+
+def fetch(fb):
+    return pl.pallas_call(
+        fetch_kernel,
+        out_shape=sds(T),
+        in_specs=[HBM],
+        out_specs=VMEM,
+        scratch_shapes=[pltpu.SemaphoreType.DMA],
+        compiler_params=pltpu.CompilerParams(vmem_limit_bytes=8 * 1024 * 1024),
+        cost_estimate=pl.CostEstimate(flops=0, bytes_accessed=1_000_000, transcendentals=0),
+    )(fb)
+
+
+def split_kernel(got, b_own, y_send, b_z):
     zl, zh = lax.axis_index("zl"), lax.axis_index("zh")
     for m in range(16):
         tile = got[m, :T, :]
@@ -72,20 +88,8 @@
         tile = got[4 * j + zl, T:, :]
         for k in range(4):
             y_send[k, 512 + j * T : 512 + (j + 1) * T, :] = tile
-    own.wait()
     for i in range(4):
-        b_z[i * T : (i + 1) * T, :] = jnp.where(zl == i, b_v[...], got[4 * zh + i, T:, :])
-
-
-def split(got, fb):
-    return pl.pallas_call(
-        split_kernel,
-        out_shape=(sds((4, CY)), sds(128)),
-        in_specs=[VMEM, HBM],
-        out_specs=(VMEM, VMEM),
-        scratch_shapes=[pltpu.VMEM((T, R), BF), pltpu.SemaphoreType.DMA],
-        compiler_params=pltpu.CompilerParams(vmem_limit_bytes=48 * 1024 * 1024),
-    )(got, fb)
+        b_z[i * T : (i + 1) * T, :] = jnp.where(zl == i, b_own[...], got[4 * zh + i, T:, :])
 
 
 def join_kernel(by_y, b_z, b_oth, x_send):
@@ -190,9 +194,9 @@
         model = lax.dot_general(ta, pair, (((1,), (1,)), ((), ())), preferred_element_type=F32)
         resids = []
         for u in range(2):
-            live = (s + u < count).astype(F32)
-            part = live * (model[u * T : (u + 1) * T, :] - obs_v[s + u].astype(F32))
-            resids.append(part.astype(BF))
+            live = (s + u < count).astype(F32).astype(BF)
+            part = model[u * T : (u + 1) * T, :] - obs_v[s + u].astype(F32)
+            resids.append(live * part.astype(BF))
             res_v[s + u] = resids[u]
         resid = jnp.concatenate(resids, axis=0)
         term_a = jnp.dot(resid, pair, preferred_element_type=F32)
@@ -264,8 +268,9 @@
     swap = [(0, 1), (1, 0)]
 
     send = spread(fa, fb, fc)
+    b_own = fetch(fb)
     got = lax.all_to_all(send, ("zh", "zl"), 0, 0, tiled=True)
-    y_send, b_z = split(got, fb)
+    y_send, b_z = small(split_kernel, (sds((4, CY)), sds(128)), got, b_own)
     by_y = lax.all_to_all(y_send, "y", 0, 0, tiled=True)
     b_oth = lax.ppermute(b_z, "co", swap)
     x_send = small(join_kernel, sds(AB), by_y, b_z, b_oth)

time: 132 us -> 131 us (level)
  the two profiles are of different devices: /device:TPU:32 before, /device:TPU:8 now
where the time goes in v4:
time: 131 us; the launch traced here: 130 us
  blocking collectives  38.4 us (29%)
  starting transfers between devices  36.9 us (28%)
  waiting for transfers between devices  36.7 us (28%)
  Pallas kernels  16.2 us (12%)
  between operations  1.39 us (1%)
    all_to_all x1, blocking collectives, on_device(): got = lax.all_to_all(send, ('zh', 'zl'), 0, 0, tiled=True)  24.1 us
    all_to_all x1, waiting for transfers between devices, on_device(): got = lax.all_to_all(send, ('zh', 'zl'), 0, 0, tiled=True)  17.6 us
    all_to_all x1, starting transfers between devices, on_device(): got = lax.all_to_all(send, ('zh', 'zl'), 0, 0, tiled=True)  15.2 us
    all_gather x1, blocking collectives, on_device(): by_x = lax.all_gather(x_send, 'x', axis=0)  14.2 us
    pallas_call x1, Pallas kernels, run_kernel(): pl.pallas_call(cp_kernel, out_shape=(jax.ShapeDtypeStruct(obs.shape, BF),...  12 us
    all_to_all x1, waiting for transfers between devices, on_device(): ab_in = lax.all_to_all(sum_ab.reshape(4, AB, R), 'x', 0, 0, tiled=True)  6.31 us
    all_to_all x1, starting transfers between devices, on_device(): by_y = lax.all_to_all(y_send, 'y', 0, 0, tiled=True)  4.91 us
    all_to_all x1, starting transfers between devices, on_device(): ca_in = lax.all_to_all(y_send, 'y', 0, 0, tiled=True)  4.91 us
  transfers between devices with their start and end apart: 8, of which 7 were waited for; matrix products, arithmetic and copies ran while one was open for 0% of the time, Pallas kernels for 0%

profile of v4, /device:TPU:8, one launch (start us, length us, event | category | flops | bytes accessed | tf_op | source)
XLA Modules:
  0.0 130.3 jit_solution(6190432578669219729)
XLA Ops:
  0.6 0.0 copy-start.1
  0.6 1.5 %shard_map.93 = bf16[16,64,128]{2,1,0:T(8,128)(2,1)} custom-call(bf16[32,128]{1,0:T(8,128)(2,1)} %bitcast.21, bf16[32,128]{1,0:T(8,128)(2,1)} %bitcast.17, bf16[32,128]{1,0:T(8,128)(2,1)} %bitcast.22), custom_call_target="tpu_custom_call" | custom-call | tf_op jit(solution)/shard_map/pallas_call | solution.py:53
  2.1 15.2 %all-to-all-start = ((bf16[16,64,128]{2,1,0:T(8,128)(2,1)}), bf16[16,64,128]{2,1,0:T(8,128)(2,1)S(1)}, u32[]{:S(2)}, u32[]{:S(2)}) async-start(bf16[16,64,128]{2,1,0:T(8,128)(2,1)} %shard_map.93), calls=%async_computation | async-start | bytes 524288 | tf_op jit(solution)/shard_map/all_to_all | solution.py:272
  17.4 0.0 copy-start
  17.4 0.7 copy-done
  18.1 17.6 %all-to-all-done.got = bf16[16,64,128]{2,1,0:T(8,128)(2,1)S(1)} async-done(((bf16[16,64,128]{2,1,0:T(8,128)(2,1)}), bf16[16,64,128]{2,1,0:T(8,128)(2,1)S(1)}, u32[]{:S(2)}, u32[]{:S(2)}) %all-to-all-start) | async-done | bytes 262176 | tf_op jit(solution)/shard_map/all_to_all | solution.py:272
  35.7 0.9 shard_map.95
  36.7 4.9 %all-to-all-start.1 = ((bf16[4,640,128]{2,1,0:T(8,128)(2,1)}), bf16[4,640,128]{2,1,0:T(8,128)(2,1)S(1)}, u32[]{:S(2)}, u32[]{:S(2)}) async-start(bf16[4,640,128]{2,1,0:T(8,128)(2,1)} %get-tuple-element.20), calls=%async_computation.1 | async-start | bytes 1310720 | tf_op jit(solution)/shard_map/all_to_all | solution.py:274
  41.6 1.9 %collective-permute-start = (bf16[128,128]{1,0:T(8,128)(2,1)S(1)}, bf16[128,128]{1,0:T(8,128)(2,1)S(1)}, u32[]{:S(2)}, u32[]{:S(2)}) collective-permute-start(bf16[128,128]{1,0:T(8,128)(2,1)S(1)} %get-tuple-element.21.b_z), channel_id=1, source_target_pairs={{0,64},{64,0},{1,65},{65,1},{2,66},{66,2},{3,67},{67,3},{4,68},{68... | collective-permute-start | bytes 98312 | tf_op jit(solution)/shard_map/ppermute | solution.py:275
  43.5 1.2 collective-permute-done.b_oth
  44.7 4.2 %all-to-all-done.1.by_y = bf16[4,640,128]{2,1,0:T(8,128)(2,1)S(1)} async-done(((bf16[4,640,128]{2,1,0:T(8,128)(2,1)}), bf16[4,640,128]{2,1,0:T(8,128)(2,1)S(1)}, u32[]{:S(2)}, u32[]{:S(2)}) %all-to-all-start.1) | async-done | bytes 655392 | tf_op jit(solution)/shard_map/all_to_all | solution.py:274
  48.9 1.9 %collective-permute-start.1 = (bf16[4,640,128]{2,1,0:T(8,128)(2,1)S(1)}, bf16[4,640,128]{2,1,0:T(8,128)(2,1)S(1)}, u32[]{:S(2)}, u32[]{:S(2)}) collective-permute-start(bf16[4,640,128]{2,1,0:T(8,128)(2,1)S(1)} %all-to-all-done.1.by_y), channel_id=1, source_target_pairs={{0,64},{64,0},{1,65},{65,1},{2,66},{66,2},{3,67},{67,3},{4,68},{68... | collective-permute-start | bytes 1966088 | tf_op jit(solution)/shard_map/ppermute | solution.py:279
  51.5 0.0 copy-done.1
  51.5 14.2 %all-gather.ab = bf16[3072,128]{1,0:T(8,128)(2,1)S(1)} all-gather(bf16[768,128]{1,0:T(8,128)(2,1)S(1)} %shard_map.96), channel_id=2, replica_groups=mesh['zl'=4,'co'=2,'zh'=4,'y'=4,'x'=4] {'x'}, dimensions={0}, use_global_device_ids=true | all-gather | bytes 983040 | tf_op jit(solution)/shard_map/all_gather | solution.py:278
  65.7 0.0 collective-permute-done.1
  65.8 12.0 %shard_map.97 = (bf16[36,32,1024]{2,1,0:T(8,128)(2,1)}, bf16[3072,128]{1,0:T(8,128)(2,1)}, f32[2048,128]{1,0:T(8,128)S(1)}, bf16[2048,128]{1,0:T(8,128)(2,1)S(1)}) custom-call(s32[3,36]{1,0:T(4,128)S(1)} %bitcast.19, s32[1]{0:T(128)} %bitcast.15.counts, bf16[3072,128]{1,0:T(8,128)(2,1)S(1)} %all-gather.ab, bf16[2560,128]{1,0:T(8,128)(2,1)S(1)} %bitcast.16, ...), custom_call_target="tpu_custom_call" | custom-call | flops 1207959552 | bytes 12000000 | tf_op jit(solution)/shard_map/pallas_call | solution.py:244
  77.8 4.2 %all-to-all-start.2 = ((bf16[4,768,128]{2,1,0:T(8,128)(2,1)}), bf16[4,768,128]{2,1,0:T(8,128)(2,1)S(1)}, u32[]{:S(2)}, u32[]{:S(2)}) async-start(bf16[4,768,128]{2,1,0:T(8,128)(2,1)} %bitcast.8), calls=%async_computation.2 | async-start | bytes 1572864 | tf_op jit(solution)/shard_map/all_to_all | solution.py:290
  82.0 1.9 %collective-permute-start.2 = (bf16[2048,128]{1,0:T(8,128)(2,1)S(1)}, bf16[2048,128]{1,0:T(8,128)(2,1)S(1)}, u32[]{:S(2)}, u32[]{:S(2)}) collective-permute-start(bf16[2048,128]{1,0:T(8,128)(2,1)S(1)} %get-tuple-element.27), channel_id=1, source_target_pairs={{0,64},{64,0},{1,65},{65,1},{2,66},{66,2},{3,67},{67,3},{4,68},{68... | collective-permute-start | bytes 1572872 | tf_op jit(solution)/shard_map/ppermute | solution.py:291
  84.0 1.9 %collective-permute-done.2.c_in = bf16[2048,128]{1,0:T(8,128)(2,1)S(1)} collective-permute-done((bf16[2048,128]{1,0:T(8,128)(2,1)S(1)}, bf16[2048,128]{1,0:T(8,128)(2,1)S(1)}, u32[]{:S(2)}, u32[]{:S(2)}) %collective-permute-start.2) | collective-permute-done | bytes 524320 | tf_op jit(solution)/shard_map/ppermute | solution.py:291
  85.8 6.3 %all-to-all-done.2.ab_in = bf16[4,768,128]{2,1,0:T(8,128)(2,1)S(1)} async-done(((bf16[4,768,128]{2,1,0:T(8,128)(2,1)}), bf16[4,768,128]{2,1,0:T(8,128)(2,1)S(1)}, u32[]{:S(2)}, u32[]{:S(2)}) %all-to-all-start.2) | async-done | bytes 786464 | tf_op jit(solution)/shard_map/all_to_all | solution.py:290
  92.2 1.0 shard_map.98
  93.1 4.9 %all-to-all-start.3 = ((bf16[4,640,128]{2,1,0:T(8,128)(2,1)}), bf16[4,640,128]{2,1,0:T(8,128)(2,1)S(1)}, u32[]{:S(2)}, u32[]{:S(2)}) async-start(bf16[4,640,128]{2,1,0:T(8,128)(2,1)} %get-tuple-element.28), calls=%async_computation.3 | async-start | bytes 1310720 | tf_op jit(solution)/shard_map/all_to_all | solution.py:295
  98.1 1.9 %collective-permute-start.3 = (bf16[128,128]{1,0:T(8,128)(2,1)S(1)}, bf16[128,128]{1,0:T(8,128)(2,1)S(1)}, u32[]{:S(2)}, u32[]{:S(2)}) collective-permute-start(bf16[128,128]{1,0:T(8,128)(2,1)S(1)} %get-tuple-element.30), channel_id=1, source_target_pairs={{0,64},{64,0},{1,65},{65,1},{2,66},{66,2},{3,67},{67,3},{4,68},{68... | collective-permute-start | bytes 98312 | tf_op jit(solution)/shard_map/ppermute | solution.py:296
  100.0 1.2 collective-permute-done.3.b_in
  101.1 4.2 %all-to-all-done.3.ca_in = bf16[4,640,128]{2,1,0:T(8,128)(2,1)S(1)} async-done(((bf16[4,640,128]{2,1,0:T(8,128)(2,1)}), bf16[4,640,128]{2,1,0:T(8,128)(2,1)S(1)}, u32[]{:S(2)}, u32[]{:S(2)}) %all-to-all-start.3) | async-done | bytes 655392 | tf_op jit(solution)/shard_map/all_to_all | solution.py:295
  105.4 0.1 shard_map.99
  105.5 24.1 %all_to_all.25.got = bf16[16,64,128]{2,1,0:T(8,128)(2,1)S(1)} all-to-all(bf16[16,64,128]{2,1,0:T(8,128)(2,1)S(1)} %get-tuple-element.31), channel_id=1, replica_groups=mesh['zl'=4,'co'=2,'zh'=4,'y'=4,'x'=4] {'zh','zl'}, dimensions={0} | all-to-all | bytes 524288 | tf_op jit(solution)/shard_map/all_to_all | solution.py:300
  129.6 0.6 shard_map.100
  (3 shorter events, 0.0 us)
Async XLA Ops:
  0.6 50.9 %copy-start.1 = (s32[3,1,1,1,36]{4,3,2,1,0:T(1,128)S(1)}, s32[3,1,1,1,36]{4,3,2,1,0:T(1,128)}, u32[]{:S(2)}) copy-start(s32[3,1,1,1,36]{4,3,2,1,0:T(1,128)} %param.10) | copy-start | bytes 1300
  2.1 33.6 %all-to-all-start = ((bf16[16,64,128]{2,1,0:T(8,128)(2,1)}), bf16[16,64,128]{2,1,0:T(8,128)(2,1)S(1)}, u32[]{:S(2)}, u32[]{:S(2)}) async-start(bf16[16,64,128]{2,1,0:T(8,128)(2,1)} %shard_map.93), calls=%async_computation | async-start | bytes 524288 | tf_op jit(solution)/shard_map/all_to_all | solution.py:272
  17.4 0.7 copy-start
  36.7 12.2 %all-to-all-start.1 = ((bf16[4,640,128]{2,1,0:T(8,128)(2,1)}), bf16[4,640,128]{2,1,0:T(8,128)(2,1)S(1)}, u32[]{:S(2)}, u32[]{:S(2)}) async-start(bf16[4,640,128]{2,1,0:T(8,128)(2,1)} %get-tuple-element.20), calls=%async_computation.1 | async-start | bytes 1310720 | tf_op jit(solution)/shard_map/all_to_all | solution.py:274
  41.6 3.1 %collective-permute-start = (bf16[128,128]{1,0:T(8,128)(2,1)S(1)}, bf16[128,128]{1,0:T(8,128)(2,1)S(1)}, u32[]{:S(2)}, u32[]{:S(2)}) collective-permute-start(bf16[128,128]{1,0:T(8,128)(2,1)S(1)} %get-tuple-element.21.b_z), channel_id=1, source_target_pairs={{0,64},{64,0},{1,65},{65,1},{2,66},{66,2},{3,67},{67,3},{4,68},{68... | collective-permute-start | bytes 98312 | tf_op jit(solution)/shard_map/ppermute | solution.py:275
  48.9 16.8 %collective-permute-start.1 = (bf16[4,640,128]{2,1,0:T(8,128)(2,1)S(1)}, bf16[4,640,128]{2,1,0:T(8,128)(2,1)S(1)}, u32[]{:S(2)}, u32[]{:S(2)}) collective-permute-start(bf16[4,640,128]{2,1,0:T(8,128)(2,1)S(1)} %all-to-all-done.1.by_y), channel_id=1, source_target_pairs={{0,64},{64,0},{1,65},{65,1},{2,66},{66,2},{3,67},{67,3},{4,68},{68... | collective-permute-start | bytes 1966088 | tf_op jit(solution)/shard_map/ppermute | solution.py:279
  77.8 14.4 %all-to-all-start.2 = ((bf16[4,768,128]{2,1,0:T(8,128)(2,1)}), bf16[4,768,128]{2,1,0:T(8,128)(2,1)S(1)}, u32[]{:S(2)}, u32[]{:S(2)}) async-start(bf16[4,768,128]{2,1,0:T(8,128)(2,1)} %bitcast.8), calls=%async_computation.2 | async-start | bytes 1572864 | tf_op jit(solution)/shard_map/all_to_all | solution.py:290
  82.0 3.8 %collective-permute-start.2 = (bf16[2048,128]{1,0:T(8,128)(2,1)S(1)}, bf16[2048,128]{1,0:T(8,128)(2,1)S(1)}, u32[]{:S(2)}, u32[]{:S(2)}) collective-permute-start(bf16[2048,128]{1,0:T(8,128)(2,1)S(1)} %get-tuple-element.27), channel_id=1, source_target_pairs={{0,64},{64,0},{1,65},{65,1},{2,66},{66,2},{3,67},{67,3},{4,68},{68... | collective-permute-start | bytes 1572872 | tf_op jit(solution)/shard_map/ppermute | solution.py:291
  93.1 12.2 %all-to-all-start.3 = ((bf16[4,640,128]{2,1,0:T(8,128)(2,1)}), bf16[4,640,128]{2,1,0:T(8,128)(2,1)S(1)}, u32[]{:S(2)}, u32[]{:S(2)}) async-start(bf16[4,640,128]{2,1,0:T(8,128)(2,1)} %get-tuple-element.28), calls=%async_computation.3 | async-start | bytes 1310720 | tf_op jit(solution)/shard_map/all_to_all | solution.py:295
  98.1 3.1 %collective-permute-start.3 = (bf16[128,128]{1,0:T(8,128)(2,1)S(1)}, bf16[128,128]{1,0:T(8,128)(2,1)S(1)}, u32[]{:S(2)}, u32[]{:S(2)}) collective-permute-start(bf16[128,128]{1,0:T(8,128)(2,1)S(1)} %get-tuple-element.30), channel_id=1, source_target_pairs={{0,64},{64,0},{1,65},{65,1},{2,66},{66,2},{3,67},{67,3},{4,68},{68... | collective-permute-start | bytes 98312 | tf_op jit(solution)/shard_map/ppermute | solution.py:296

commit v5 on v4

--- a/solution.py
+++ b/solution.py
@@ -9,7 +9,7 @@
 F32 = jnp.float32
 T = 32
 R = 128
-UNROLL = 36
+CHUNK = 12
 VMEM = pl.BlockSpec(memory_space=pltpu.VMEM)
 SMEM = pl.BlockSpec(memory_space=pltpu.SMEM)
 HBM = pl.BlockSpec(memory_space=pltpu.HBM)
@@ -149,19 +149,19 @@
 def cp_kernel(pos, counts, ab, own, oth, obs, res, out_ab, out_own, out_oth,
               acc_ab, acc, obs_v, res_v, in_sem, out_sem):
     slots = obs.shape[0]
-    groups = slots // UNROLL
+    chunks = slots // CHUNK
     co = lax.axis_index("co")
     count = counts[0]
 
     def load(g):
-        part = pl.ds(g * UNROLL, UNROLL)
+        part = pl.ds(g * CHUNK, CHUNK)
         return pltpu.make_async_copy(obs.at[part], obs_v.at[part], in_sem.at[g])
 
     def store(g):
-        part = pl.ds(g * UNROLL, UNROLL)
+        part = pl.ds(g * CHUNK, CHUNK)
         return pltpu.make_async_copy(res_v.at[part], res.at[part], out_sem.at[g])
 
-    for g in range(groups):
+    for g in range(chunks):
         load(g).start()
     acc_ab[...] = jnp.zeros_like(acc_ab)
     acc[...] = jnp.zeros_like(acc)
@@ -210,37 +210,29 @@
             for u in range(2)
         ]
 
-    def group(g, carry):
-        base = g * UNROLL
+    found = []
+    for g in range(chunks):
         load(g).wait()
-
-        @pl.when(base < count)
-        def _():
-            found = [t for u in range(0, UNROLL, 2) for t in two(base + u)]
-            for u, (term_a, term_b, term_c) in enumerate(found):
-                at_a, at_b, y, in_plane, other = places(base + u)
-                acc_ab[rows(at_a), :] += term_a
-                acc_ab[rows(at_b), :] += term_b
-                acc[rows(other * 2048 + y * 512 + in_plane), :] += term_c
-
-        @pl.when(base >= count)
-        def _():
-            res_v[pl.ds(base, UNROLL)] = jnp.zeros((UNROLL,) + res.shape[1:], BF)
-
+    for g in range(chunks):
+        for u in range(0, CHUNK, 2):
+            found += two(g * CHUNK + u)
         store(g).start()
-        return carry
-
-    lax.fori_loop(0, groups, group, 0)
+    for s, (term_a, term_b, term_c) in enumerate(found):
+        at_a, at_b, y, in_plane, other = places(s)
+        acc_ab[rows(at_a), :] += term_a
+        acc_ab[rows(at_b), :] += term_b
+        acc[rows(other * 2048 + y * 512 + in_plane), :] += term_c
+
     out_ab[...] = acc_ab[...].astype(BF)
     out_own[...] = acc[:2048, :]
     out_oth[...] = acc[2048:, :].astype(BF)
-    for g in range(groups):
+    for g in range(chunks):
         store(g).wait()
 
 
 def run_kernel(pos, counts, ab, own, oth, obs):
     slots = obs.shape[0]
-    groups = slots // UNROLL
+    chunks = slots // CHUNK
     return pl.pallas_call(
         cp_kernel,
         out_shape=(jax.ShapeDtypeStruct(obs.shape, BF),
@@ -252,8 +244,8 @@
             pltpu.VMEM((4096, R), F32),
             pltpu.VMEM(obs.shape, BF),
             pltpu.VMEM(obs.shape, BF),
-            pltpu.SemaphoreType.DMA((groups,)),
-            pltpu.SemaphoreType.DMA((groups,)),
+            pltpu.SemaphoreType.DMA((chunks,)),
+            pltpu.SemaphoreType.DMA((chunks,)),
         ],
         compiler_params=pltpu.CompilerParams(vmem_limit_bytes=48 * 1024 * 1024),
         cost_estimate=pl.CostEstimate(

time: 131 us -> 130 us (level)
  no operation moved by 1% of the time
where the time goes in v5:
time: 130 us
  blocking collectives  38.4 us (30%)
  starting transfers between devices  36.9 us (28%)
  waiting for transfers between devices  36.7 us (28%)
  Pallas kernels  15.7 us (12%)
  between operations  1.39 us (1%)
    all_to_all x1, blocking collectives, on_device(): got = lax.all_to_all(send, ('zh', 'zl'), 0, 0, tiled=True)  24.1 us
    all_to_all x1, waiting for transfers between devices, on_device(): got = lax.all_to_all(send, ('zh', 'zl'), 0, 0, tiled=True)  17.6 us
    all_to_all x1, starting transfers between devices, on_device(): got = lax.all_to_all(send, ('zh', 'zl'), 0, 0, tiled=True)  15.2 us
    all_gather x1, blocking collectives, on_device(): by_x = lax.all_gather(x_send, 'x', axis=0)  14.2 us
    pallas_call x1, Pallas kernels, run_kernel(): pl.pallas_call(cp_kernel, out_shape=(jax.ShapeDtypeStruct(obs.shape, BF),...  11.5 us
    all_to_all x1, waiting for transfers between devices, on_device(): ab_in = lax.all_to_all(sum_ab.reshape(4, AB, R), 'x', 0, 0, tiled=True)  6.32 us
    all_to_all x1, starting transfers between devices, on_device(): by_y = lax.all_to_all(y_send, 'y', 0, 0, tiled=True)  4.91 us
    all_to_all x1, starting transfers between devices, on_device(): ca_in = lax.all_to_all(y_send, 'y', 0, 0, tiled=True)  4.9 us
  transfers between devices with their start and end apart: 8, of which 7 were waited for; matrix products, arithmetic and copies ran while one was open for 0% of the time, Pallas kernels for 0%

profile of v5, /device:TPU:8, one launch (start us, length us, event | category | flops | bytes accessed | tf_op | source)
XLA Modules:
  0.0 129.7 jit_solution(6707504426851756784)
XLA Ops:
  0.6 0.0 copy-start.1
  0.6 1.5 %shard_map.93 = bf16[16,64,128]{2,1,0:T(8,128)(2,1)} custom-call(bf16[32,128]{1,0:T(8,128)(2,1)} %bitcast.21, bf16[32,128]{1,0:T(8,128)(2,1)} %bitcast.17, bf16[32,128]{1,0:T(8,128)(2,1)} %bitcast.22), custom_call_target="tpu_custom_call" | custom-call | tf_op jit(solution)/shard_map/pallas_call | solution.py:53
  2.1 15.2 %all-to-all-start = ((bf16[16,64,128]{2,1,0:T(8,128)(2,1)}), bf16[16,64,128]{2,1,0:T(8,128)(2,1)S(1)}, u32[]{:S(2)}, u32[]{:S(2)}) async-start(bf16[16,64,128]{2,1,0:T(8,128)(2,1)} %shard_map.93), calls=%async_computation | async-start | bytes 524288 | tf_op jit(solution)/shard_map/all_to_all | solution.py:264
  17.4 0.0 copy-start
  17.4 0.7 copy-done
  18.1 17.6 %all-to-all-done.got = bf16[16,64,128]{2,1,0:T(8,128)(2,1)S(1)} async-done(((bf16[16,64,128]{2,1,0:T(8,128)(2,1)}), bf16[16,64,128]{2,1,0:T(8,128)(2,1)S(1)}, u32[]{:S(2)}, u32[]{:S(2)}) %all-to-all-start) | async-done | bytes 262176 | tf_op jit(solution)/shard_map/all_to_all | solution.py:264
  35.7 0.9 shard_map.95
  36.7 4.9 %all-to-all-start.1 = ((bf16[4,640,128]{2,1,0:T(8,128)(2,1)}), bf16[4,640,128]{2,1,0:T(8,128)(2,1)S(1)}, u32[]{:S(2)}, u32[]{:S(2)}) async-start(bf16[4,640,128]{2,1,0:T(8,128)(2,1)} %get-tuple-element.20), calls=%async_computation.1 | async-start | bytes 1310720 | tf_op jit(solution)/shard_map/all_to_all | solution.py:266
  41.6 1.9 %collective-permute-start = (bf16[128,128]{1,0:T(8,128)(2,1)S(1)}, bf16[128,128]{1,0:T(8,128)(2,1)S(1)}, u32[]{:S(2)}, u32[]{:S(2)}) collective-permute-start(bf16[128,128]{1,0:T(8,128)(2,1)S(1)} %get-tuple-element.21.b_z), channel_id=1, source_target_pairs={{0,64},{64,0},{1,65},{65,1},{2,66},{66,2},{3,67},{67,3},{4,68},{68... | collective-permute-start | bytes 98312 | tf_op jit(solution)/shard_map/ppermute | solution.py:267
  43.5 1.2 collective-permute-done.b_oth
  44.7 4.2 %all-to-all-done.1.by_y = bf16[4,640,128]{2,1,0:T(8,128)(2,1)S(1)} async-done(((bf16[4,640,128]{2,1,0:T(8,128)(2,1)}), bf16[4,640,128]{2,1,0:T(8,128)(2,1)S(1)}, u32[]{:S(2)}, u32[]{:S(2)}) %all-to-all-start.1) | async-done | bytes 655392 | tf_op jit(solution)/shard_map/all_to_all | solution.py:266
  48.9 1.9 %collective-permute-start.1 = (bf16[4,640,128]{2,1,0:T(8,128)(2,1)S(1)}, bf16[4,640,128]{2,1,0:T(8,128)(2,1)S(1)}, u32[]{:S(2)}, u32[]{:S(2)}) collective-permute-start(bf16[4,640,128]{2,1,0:T(8,128)(2,1)S(1)} %all-to-all-done.1.by_y), channel_id=1, source_target_pairs={{0,64},{64,0},{1,65},{65,1},{2,66},{66,2},{3,67},{67,3},{4,68},{68... | collective-permute-start | bytes 1966088 | tf_op jit(solution)/shard_map/ppermute | solution.py:271
  51.5 0.0 copy-done.1
  51.5 14.2 %all-gather.ab = bf16[3072,128]{1,0:T(8,128)(2,1)S(1)} all-gather(bf16[768,128]{1,0:T(8,128)(2,1)S(1)} %shard_map.96), channel_id=2, replica_groups=mesh['zl'=4,'co'=2,'zh'=4,'y'=4,'x'=4] {'x'}, dimensions={0}, use_global_device_ids=true | all-gather | bytes 983040 | tf_op jit(solution)/shard_map/all_gather | solution.py:270
  65.7 0.0 collective-permute-done.1
  65.8 11.5 %shard_map.97 = (bf16[36,32,1024]{2,1,0:T(8,128)(2,1)}, bf16[3072,128]{1,0:T(8,128)(2,1)}, f32[2048,128]{1,0:T(8,128)S(1)}, bf16[2048,128]{1,0:T(8,128)(2,1)S(1)}) custom-call(s32[3,36]{1,0:T(4,128)S(1)} %bitcast.19, s32[1]{0:T(128)} %bitcast.15.counts, bf16[3072,128]{1,0:T(8,128)(2,1)S(1)} %all-gather.ab, bf16[2560,128]{1,0:T(8,128)(2,1)S(1)} %bitcast.16, ...), custom_call_target="tpu_custom_call" | custom-call | flops 1207959552 | bytes 12000000 | tf_op jit(solution)/shard_map/pallas_call | solution.py:236
  77.2 4.2 %all-to-all-start.2 = ((bf16[4,768,128]{2,1,0:T(8,128)(2,1)}), bf16[4,768,128]{2,1,0:T(8,128)(2,1)S(1)}, u32[]{:S(2)}, u32[]{:S(2)}) async-start(bf16[4,768,128]{2,1,0:T(8,128)(2,1)} %bitcast.8), calls=%async_computation.2 | async-start | bytes 1572864 | tf_op jit(solution)/shard_map/all_to_all | solution.py:282
  81.5 1.9 %collective-permute-start.2 = (bf16[2048,128]{1,0:T(8,128)(2,1)S(1)}, bf16[2048,128]{1,0:T(8,128)(2,1)S(1)}, u32[]{:S(2)}, u32[]{:S(2)}) collective-permute-start(bf16[2048,128]{1,0:T(8,128)(2,1)S(1)} %get-tuple-element.27), channel_id=1, source_target_pairs={{0,64},{64,0},{1,65},{65,1},{2,66},{66,2},{3,67},{67,3},{4,68},{68... | collective-permute-start | bytes 1572872 | tf_op jit(solution)/shard_map/ppermute | solution.py:283
  83.4 1.9 %collective-permute-done.2.c_in = bf16[2048,128]{1,0:T(8,128)(2,1)S(1)} collective-permute-done((bf16[2048,128]{1,0:T(8,128)(2,1)S(1)}, bf16[2048,128]{1,0:T(8,128)(2,1)S(1)}, u32[]{:S(2)}, u32[]{:S(2)}) %collective-permute-start.2) | collective-permute-done | bytes 524320 | tf_op jit(solution)/shard_map/ppermute | solution.py:283
  85.3 6.3 %all-to-all-done.2.ab_in = bf16[4,768,128]{2,1,0:T(8,128)(2,1)S(1)} async-done(((bf16[4,768,128]{2,1,0:T(8,128)(2,1)}), bf16[4,768,128]{2,1,0:T(8,128)(2,1)S(1)}, u32[]{:S(2)}, u32[]{:S(2)}) %all-to-all-start.2) | async-done | bytes 786464 | tf_op jit(solution)/shard_map/all_to_all | solution.py:282
  91.6 1.0 shard_map.98
  92.6 4.9 %all-to-all-start.3 = ((bf16[4,640,128]{2,1,0:T(8,128)(2,1)}), bf16[4,640,128]{2,1,0:T(8,128)(2,1)S(1)}, u32[]{:S(2)}, u32[]{:S(2)}) async-start(bf16[4,640,128]{2,1,0:T(8,128)(2,1)} %get-tuple-element.28), calls=%async_computation.3 | async-start | bytes 1310720 | tf_op jit(solution)/shard_map/all_to_all | solution.py:287
  97.5 1.9 %collective-permute-start.3 = (bf16[128,128]{1,0:T(8,128)(2,1)S(1)}, bf16[128,128]{1,0:T(8,128)(2,1)S(1)}, u32[]{:S(2)}, u32[]{:S(2)}) collective-permute-start(bf16[128,128]{1,0:T(8,128)(2,1)S(1)} %get-tuple-element.30), channel_id=1, source_target_pairs={{0,64},{64,0},{1,65},{65,1},{2,66},{66,2},{3,67},{67,3},{4,68},{68... | collective-permute-start | bytes 98312 | tf_op jit(solution)/shard_map/ppermute | solution.py:288
  99.4 1.2 collective-permute-done.3.b_in
  100.6 4.2 %all-to-all-done.3.ca_in = bf16[4,640,128]{2,1,0:T(8,128)(2,1)S(1)} async-done(((bf16[4,640,128]{2,1,0:T(8,128)(2,1)}), bf16[4,640,128]{2,1,0:T(8,128)(2,1)S(1)}, u32[]{:S(2)}, u32[]{:S(2)}) %all-to-all-start.3) | async-done | bytes 655392 | tf_op jit(solution)/shard_map/all_to_all | solution.py:287
  104.8 0.1 shard_map.99
  104.9 24.1 %all_to_all.25.got = bf16[16,64,128]{2,1,0:T(8,128)(2,1)S(1)} all-to-all(bf16[16,64,128]{2,1,0:T(8,128)(2,1)S(1)} %get-tuple-element.31), channel_id=1, replica_groups=mesh['zl'=4,'co'=2,'zh'=4,'y'=4,'x'=4] {'zh','zl'}, dimensions={0} | all-to-all | bytes 524288 | tf_op jit(solution)/shard_map/all_to_all | solution.py:292
  129.0 0.6 shard_map.100
  (3 shorter events, 0.0 us)
Async XLA Ops:
  0.6 50.9 %copy-start.1 = (s32[3,1,1,1,36]{4,3,2,1,0:T(1,128)S(1)}, s32[3,1,1,1,36]{4,3,2,1,0:T(1,128)}, u32[]{:S(2)}) copy-start(s32[3,1,1,1,36]{4,3,2,1,0:T(1,128)} %param.10) | copy-start | bytes 1300
  2.1 33.6 %all-to-all-start = ((bf16[16,64,128]{2,1,0:T(8,128)(2,1)}), bf16[16,64,128]{2,1,0:T(8,128)(2,1)S(1)}, u32[]{:S(2)}, u32[]{:S(2)}) async-start(bf16[16,64,128]{2,1,0:T(8,128)(2,1)} %shard_map.93), calls=%async_computation | async-start | bytes 524288 | tf_op jit(solution)/shard_map/all_to_all | solution.py:264
  17.4 0.7 copy-start
  36.7 12.2 %all-to-all-start.1 = ((bf16[4,640,128]{2,1,0:T(8,128)(2,1)}), bf16[4,640,128]{2,1,0:T(8,128)(2,1)S(1)}, u32[]{:S(2)}, u32[]{:S(2)}) async-start(bf16[4,640,128]{2,1,0:T(8,128)(2,1)} %get-tuple-element.20), calls=%async_computation.1 | async-start | bytes 1310720 | tf_op jit(solution)/shard_map/all_to_all | solution.py:266
  41.6 3.1 %collective-permute-start = (bf16[128,128]{1,0:T(8,128)(2,1)S(1)}, bf16[128,128]{1,0:T(8,128)(2,1)S(1)}, u32[]{:S(2)}, u32[]{:S(2)}) collective-permute-start(bf16[128,128]{1,0:T(8,128)(2,1)S(1)} %get-tuple-element.21.b_z), channel_id=1, source_target_pairs={{0,64},{64,0},{1,65},{65,1},{2,66},{66,2},{3,67},{67,3},{4,68},{68... | collective-permute-start | bytes 98312 | tf_op jit(solution)/shard_map/ppermute | solution.py:267
  48.9 16.8 %collective-permute-start.1 = (bf16[4,640,128]{2,1,0:T(8,128)(2,1)S(1)}, bf16[4,640,128]{2,1,0:T(8,128)(2,1)S(1)}, u32[]{:S(2)}, u32[]{:S(2)}) collective-permute-start(bf16[4,640,128]{2,1,0:T(8,128)(2,1)S(1)} %all-to-all-done.1.by_y), channel_id=1, source_target_pairs={{0,64},{64,0},{1,65},{65,1},{2,66},{66,2},{3,67},{67,3},{4,68},{68... | collective-permute-start | bytes 1966088 | tf_op jit(solution)/shard_map/ppermute | solution.py:271
  77.2 14.4 %all-to-all-start.2 = ((bf16[4,768,128]{2,1,0:T(8,128)(2,1)}), bf16[4,768,128]{2,1,0:T(8,128)(2,1)S(1)}, u32[]{:S(2)}, u32[]{:S(2)}) async-start(bf16[4,768,128]{2,1,0:T(8,128)(2,1)} %bitcast.8), calls=%async_computation.2 | async-start | bytes 1572864 | tf_op jit(solution)/shard_map/all_to_all | solution.py:282
  81.5 3.8 %collective-permute-start.2 = (bf16[2048,128]{1,0:T(8,128)(2,1)S(1)}, bf16[2048,128]{1,0:T(8,128)(2,1)S(1)}, u32[]{:S(2)}, u32[]{:S(2)}) collective-permute-start(bf16[2048,128]{1,0:T(8,128)(2,1)S(1)} %get-tuple-element.27), channel_id=1, source_target_pairs={{0,64},{64,0},{1,65},{65,1},{2,66},{66,2},{3,67},{67,3},{4,68},{68... | collective-permute-start | bytes 1572872 | tf_op jit(solution)/shard_map/ppermute | solution.py:283
  92.6 12.2 %all-to-all-start.3 = ((bf16[4,640,128]{2,1,0:T(8,128)(2,1)}), bf16[4,640,128]{2,1,0:T(8,128)(2,1)S(1)}, u32[]{:S(2)}, u32[]{:S(2)}) async-start(bf16[4,640,128]{2,1,0:T(8,128)(2,1)} %get-tuple-element.28), calls=%async_computation.3 | async-start | bytes 1310720 | tf_op jit(solution)/shard_map/all_to_all | solution.py:287
  97.5 3.1 %collective-permute-start.3 = (bf16[128,128]{1,0:T(8,128)(2,1)S(1)}, bf16[128,128]{1,0:T(8,128)(2,1)S(1)}, u32[]{:S(2)}, u32[]{:S(2)}) collective-permute-start(bf16[128,128]{1,0:T(8,128)(2,1)S(1)} %get-tuple-element.30), channel_id=1, source_target_pairs={{0,64},{64,0},{1,65},{65,1},{2,66},{66,2},{3,67},{67,3},{4,68},{68... | collective-permute-start | bytes 98312 | tf_op jit(solution)/shard_map/ppermute | solution.py:288
